TPU v7x, 32 devices: a whole 2x2x4 slice. The times are simulated.
32 devices in a mesh: grp: 2 (over x), inst: 8 (over z, y), tp: 2 (over core).
Axes of the slice: x: 2, y: 2, z: 4, core: 2. Of those that a mesh axis runs over, the one named last changes fastest.
Arguments:
- tokens: bfloat16 [2, 2560, 4096], P(None, ('grp', 'inst'), 'tp'), parts along dimension 1, may hold values from -6 to 6
- queries: bfloat16 [2, 2560, 8192], P(None, ('grp', 'inst'), 'tp'), parts along dimension 1, may hold values from -100 to 100
- key_value_cache: bfloat16 [2560, 8, 2, 1024], P(('grp', 'inst'), None, None, 'tp'), parts along dimension 0, may hold values from -4 to 4
- key_value_length: int32 [2560], P(('grp', 'inst')), parts along dimension 0, may hold values from 2 to 8, as said below
- request_adapter_index: int32 [2560, 1], P(('grp', 'inst')), parts along dimension 0, may hold values from 0 to 7; in each aligned block of 160 rows (0 to 159, 160 to 319, ...) at most 24 rows name the same one
- adapter_destination: int32 [128], P('grp'), parts along dimension 0, may hold values from 0 to 7, as said below
- key_matrix: bfloat16 [4096, 1024], P('tp'), may hold values from -0.09375 to 0.09375
- value_matrix: bfloat16 [4096, 1024], P('tp'), may hold values from -0.09375 to 0.09375
- adapter_down_maps: bfloat16 [128, 4096, 128], P(('grp', 'inst'), 'tp'), parts along dimension 0, may hold values from -0.09375 to 0.09375
- adapter_up_maps: bfloat16 [128, 2, 64, 1024], P(('grp', 'inst'), None, None, 'tp'), parts along dimension 0, may hold values from -0.75 to 0.75
Outputs:
- attended: bfloat16 [2, 3072, 8192], P(None, ('grp', 'inst'), 'tp'), parts along dimension 1
- new_kv: bfloat16 [2, 3072, 2, 1024], P(None, ('grp', 'inst'), None, 'tp'), parts along dimension 1
There are 2 independent parts, one for each index of `grp`. A program takes and returns all parts, laid end to end along the dimension named above; an argument that names none is the same for every part. Nothing has to cross between parts.
Inputs may be any that keep to these rules, and one draw needn't show every extreme that they name: `adapter_destination`: each instance is the destination of exactly 8 adapters, at most one of them from any one instance (its own included). `key_value_length`: every instance holds a request with exactly 8 live positions. `request_adapter_index`: among one instance's 160 requests at most 24 use the same adapter, and some adapter has exactly 24.
All inputs are finite; a program needn't handle non-finite values.
Results may differ from a plain program's by a relative error of at most 0.0065.
Values may be sent and summed in bfloat16 or wider, within the bound.
A program may use at most 192 MiB of HBM per device.

v0:
```python
import jax
import jax.numpy as jnp
from jax import lax
from jax.sharding import PartitionSpec as P

QUERY_GROUP = 8
HEAD_SIZE = 128
SEG = 24


def project_slots(
    tokens_seg, queries_seg, cache_seg, lengths_seg, adapt_down, adapt_up, key_matrix, value_matrix
):
    slot_count, count_steps, seg_rows, feature_part = tokens_seg.shape
    key_part = cache_seg.shape[-1]
    query_part = queries_seg.shape[-1]
    rank_half = adapt_down.shape[-1] // 2
    head_local = key_part // HEAD_SIZE
    flat_tokens = tokens_seg.reshape(-1, feature_part)
    partial_key = jnp.dot(flat_tokens, key_matrix, preferred_element_type=jnp.float32)
    partial_value = jnp.dot(flat_tokens, value_matrix, preferred_element_type=jnp.float32)
    partial_value = jnp.stack([partial_key, partial_value], axis=1)
    lowpart = jnp.einsum(
        "smd,sdk->smk",
        tokens_seg.reshape(slot_count, -1, feature_part),
        adapt_down,
        preferred_element_type=jnp.float32,
    )
    own_base = lax.psum_scatter(partial_value, "tp", scatter_dimension=2, tiled=True)
    low_total = lax.psum(lowpart, "tp")
    low_round = low_total.astype(jnp.bfloat16).reshape(slot_count, -1, 2, rank_half)
    adapter_term = jnp.einsum(
        "smcr,scrk->smck", low_round, adapt_up, preferred_element_type=jnp.float32
    )
    fresh_kv = (own_base.reshape(slot_count, -1, 2, key_part) + adapter_term).astype(jnp.bfloat16)
    fresh_kv = fresh_kv.reshape(slot_count, count_steps, seg_rows, 2, key_part)
    query_head_rows = queries_seg.reshape(
        slot_count, count_steps, seg_rows, head_local, QUERY_GROUP, HEAD_SIZE
    )
    previous_keys = cache_seg[:, :, :, 0].reshape(slot_count, seg_rows, -1, head_local, HEAD_SIZE)
    previous_values = cache_seg[:, :, :, 1].reshape(slot_count, seg_rows, -1, head_local, HEAD_SIZE)
    appended_keys = fresh_kv[:, :, :, 0].reshape(
        slot_count, count_steps, seg_rows, head_local, HEAD_SIZE
    )
    appended_values = fresh_kv[:, :, :, 1].reshape(
        slot_count, count_steps, seg_rows, head_local, HEAD_SIZE
    )
    factor = HEAD_SIZE ** (-0.5)
    old_scores = (
        jnp.einsum(
            "stnghd,snpgd->stnghp",
            query_head_rows,
            previous_keys,
            preferred_element_type=jnp.float32,
        )
        * factor
    )
    positions = jnp.arange(previous_keys.shape[2])
    visible = positions[None, None, :] < lengths_seg[:, :, None]
    old_scores = jnp.where(visible[:, None, :, None, None, :], old_scores, -jnp.inf)
    new_scores = (
        jnp.einsum(
            "stnghd,sungd->stnghu",
            query_head_rows,
            appended_keys,
            preferred_element_type=jnp.float32,
        )
        * factor
    )
    causal = jnp.arange(count_steps)[None, :] <= jnp.arange(count_steps)[:, None]
    new_scores = jnp.where(causal[None, :, None, None, None, :], new_scores, -jnp.inf)
    highest = jnp.maximum(jnp.max(old_scores, axis=-1), jnp.max(new_scores, axis=-1))[..., None]
    old_exp = jnp.exp(old_scores - highest)
    new_exp = jnp.exp(new_scores - highest)
    normaliser = jnp.sum(old_exp, axis=-1, keepdims=True) + jnp.sum(new_exp, axis=-1, keepdims=True)
    old_weights = (old_exp / normaliser).astype(jnp.bfloat16)
    new_weights = (new_exp / normaliser).astype(jnp.bfloat16)
    served = jnp.einsum(
        "stnghp,snpgd->stnghd", old_weights, previous_values, preferred_element_type=jnp.float32
    )
    served = served + jnp.einsum(
        "stnghu,sungd->stnghd", new_weights, appended_values, preferred_element_type=jnp.float32
    )
    living = lengths_seg > 0
    served = jnp.where(living[:, None, :, None, None, None], served, 0.0).astype(jnp.bfloat16)
    served = served.reshape(slot_count, count_steps, seg_rows, query_part)
    fresh_kv = jnp.where(living[:, None, :, None, None], fresh_kv, jnp.zeros((), jnp.bfloat16))
    return (served, fresh_kv)


def on_device(
    tokens,
    queries,
    key_value_cache,
    key_value_length,
    request_adapter_index,
    adapter_destination,
    key_matrix,
    value_matrix,
    adapter_down_maps,
    adapter_up_maps,
):
    slot_count = adapter_down_maps.shape[0]
    home_rows = request_adapter_index.shape[0]
    count_steps = tokens.shape[0]
    instances = lax.axis_size("inst")
    own_index = lax.axis_index("inst")
    chosen_adapter = request_adapter_index[:, 0]
    member = (chosen_adapter[:, None] == jnp.arange(slot_count)[None, :]).astype(jnp.int32)
    within = jnp.sum((jnp.cumsum(member, axis=0) - 1) * member, axis=1)
    seat_index = chosen_adapter * SEG + within
    pairing = (seat_index[None, :] == jnp.arange(slot_count * SEG)[:, None]).astype(jnp.int32)
    source = jnp.sum(pairing * jnp.arange(home_rows)[None, :], axis=1)
    filled = jnp.sum(pairing, axis=1)
    lengths = (jnp.take(key_value_length, source) * filled).reshape(slot_count, SEG)
    seg_tokens = jnp.swapaxes(
        jnp.take(tokens, source, axis=1).reshape(count_steps, slot_count, SEG, -1), 0, 1
    )
    seg_queries = jnp.swapaxes(
        jnp.take(queries, source, axis=1).reshape(count_steps, slot_count, SEG, -1), 0, 1
    )
    seg_cache = jnp.take(key_value_cache, source, axis=0).reshape(
        (slot_count, SEG) + key_value_cache.shape[1:]
    )
    leaving = lax.dynamic_slice_in_dim(adapter_destination, own_index * slot_count, slot_count)
    toward = (leaving[None, :] == jnp.arange(instances)[:, None]).astype(jnp.int32)
    picked_slot = jnp.sum(toward * jnp.arange(slot_count)[None, :], axis=1)
    present = jnp.sum(toward, axis=1)
    arriving = jnp.sum(
        (adapter_destination.reshape(instances, slot_count) == own_index).astype(jnp.int32), axis=1
    )
    ranking = jnp.cumsum(arriving) - 1
    selector = arriving[None, :] * (ranking[None, :] == jnp.arange(slot_count)[:, None]).astype(
        jnp.int32
    )
    anchor = jnp.sum(selector * jnp.arange(instances)[None, :], axis=1)

    def outgoing_adapters(payload):
        selected = jnp.take(payload, picked_slot, axis=0)
        retain = present.reshape((-1,) + (1,) * (payload.ndim - 1)).astype(payload.dtype)
        return selected * retain

    def inward(payload):
        return jnp.take(payload, anchor, axis=0)

    arrived = (
        lax.all_to_all(
            outgoing_adapters(adapter_down_maps), "inst", split_axis=0, concat_axis=0, tiled=True
        ),
        lax.all_to_all(
            outgoing_adapters(adapter_up_maps), "inst", split_axis=0, concat_axis=0, tiled=True
        ),
        lax.all_to_all(
            outgoing_adapters(seg_tokens), "inst", split_axis=0, concat_axis=0, tiled=True
        ),
        lax.all_to_all(
            outgoing_adapters(seg_queries), "inst", split_axis=0, concat_axis=0, tiled=True
        ),
        lax.all_to_all(
            outgoing_adapters(seg_cache), "inst", split_axis=0, concat_axis=0, tiled=True
        ),
        lax.all_to_all(
            outgoing_adapters(lengths.astype(jnp.bfloat16)),
            "inst",
            split_axis=0,
            concat_axis=0,
            tiled=True,
        ),
    )
    served, fresh_kv = project_slots(
        inward(arrived[2]),
        inward(arrived[3]),
        inward(arrived[4]),
        inward(arrived[5]).astype(jnp.int32),
        inward(arrived[0]),
        inward(arrived[1]),
        key_matrix,
        value_matrix,
    )
    attended = jnp.swapaxes(served, 0, 1).reshape(count_steps, slot_count * SEG, -1)
    renewed = jnp.swapaxes(fresh_kv, 0, 1).reshape(count_steps, slot_count * SEG, 2, -1)
    return (attended, renewed)


def solution(mesh):
    return jax.shard_map(
        on_device,
        mesh=mesh,
        in_specs=(
            P(None, ("grp", "inst"), "tp"),
            P(None, ("grp", "inst"), "tp"),
            P(("grp", "inst"), None, None, "tp"),
            P(("grp", "inst")),
            P(("grp", "inst"), None),
            P("grp"),
            P("tp", None),
            P("tp", None),
            P(("grp", "inst"), "tp", None),
            P(("grp", "inst"), None, None, "tp"),
        ),
        out_specs=(P(None, ("grp", "inst"), "tp"), P(None, ("grp", "inst"), None, "tp")),
        check_vma=False,
    )
```

profile of v0, /device:TPU:0, one launch (start us, length us, event | category | flops | bytes accessed | tf_op | source)
XLA Modules:
  0.0 413.3 jit_solution(13140261783118759225)
XLA Ops:
  7.2 0.9 dynamic_slice.3
  8.3 0.7 iota_compare_fusion.2
  9.0 0.6 reduce-window.18
  9.9 0.7 fusion.26
  10.6 0.7 multiply_add_fusion
  11.5 2.0 gather_fusion
  13.7 0.6 gather_fusion.4
  14.3 0.6 copy.80
  14.9 7.3 %all-to-all-start = ((bf16[8,1,24]{2,1,0:T(2,128)(2,1)}), bf16[8,1,24]{2,1,0:T(2,128)(2,1)S(1)}, u32[]{:S(2)}, u32[]{:S(2)}) async-start(bf16[8,1,24]{2,1,0:T(2,128)(2,1)} %copy.80), calls=%async_computation | async-start | bytes 8192 | tf_op jit(solution)/shard_map/all_to_all | solution.py:162
  22.2 2.8 gather_fusion.12
  25.0 2.4 select_multiply_fusion.4
  27.4 1.2 all-to-all-done
  28.6 4.8 %all-to-all-start.4 = ((bf16[8,2,64,512]{3,2,1,0:T(8,128)(2,1)}), bf16[8,2,64,512]{3,2,1,0:T(8,128)(2,1)}, u32[]{:S(2)}, u32[]{:S(2)}) async-start(bf16[8,2,64,512]{3,2,1,0:T(8,128)(2,1)} %select_multiply_fusion.4), calls=%async_computation.5 | async-start | bytes 2097152 | tf_op jit(solution)/shard_map/all_to_all | solution.py:150
  33.4 11.9 %gather_fusion.3 = bf16[192,2,2048]{2,0,1:T(8,128)(2,1)} fusion(bf16[2,160,2048]{2,1,0:T(8,128)(2,1)} %param.22, s32[1024]{0:T(1024)S(1)} %pad_clamp_fusion.2), kind=kCustom, calls=%fused_computation.15 | custom fusion | bytes 3146496 | tf_op jit(solution)/shard_map/jit(_take)/gather | solution.py:117
  45.3 2.8 select_bitcast_fusion.1
  48.0 3.2 gather_fusion.10
  51.2 2.8 select_multiply_fusion.3
  54.0 4.9 %all-to-all-done.4 = bf16[8,2,64,512]{3,2,1,0:T(8,128)(2,1)} async-done(((bf16[8,2,64,512]{3,2,1,0:T(8,128)(2,1)}), bf16[8,2,64,512]{3,2,1,0:T(8,128)(2,1)}, u32[]{:S(2)}, u32[]{:S(2)}) %all-to-all-start.4) | async-done | bytes 1048608 | tf_op jit(solution)/shard_map/all_to_all | solution.py:150
  58.9 4.5 %all-to-all-start.3 = ((bf16[8,2,24,2048]{3,2,1,0:T(8,128)(2,1)}), bf16[8,2,24,2048]{3,2,1,0:T(8,128)(2,1)}, u32[]{:S(2)}, u32[]{:S(2)}) async-start(bf16[8,2,24,2048]{3,2,1,0:T(8,128)(2,1)} %select_multiply_fusion.3), calls=%async_computation.3 | async-start | bytes 3145728 | tf_op jit(solution)/shard_map/all_to_all | solution.py:153
  63.4 15.0 %gather_fusion.2 = bf16[192,2,4096]{2,0,1:T(8,128)(2,1)} fusion(bf16[2,160,4096]{2,1,0:T(8,128)(2,1)S(1)} %copy-done, s32[1024]{0:T(1024)S(1)} %pad_clamp_fusion.2), kind=kCustom, calls=%fused_computation.14 | custom fusion | bytes 6292224 | tf_op jit(solution)/shard_map/jit(_take)/gather | solution.py:120
  78.4 3.9 select_bitcast_fusion
  82.3 4.3 %gather_fusion.8 = bf16[8,2,24,4096]{3,2,1,0:T(8,128)(2,1)} fusion(bf16[8,2,24,4096]{3,2,0,1:T(8,128)(2,1)} %select_bitcast_fusion, s32[1024]{0:T(1024)S(1)} %pad_clamp_fusion.1), kind=kCustom, calls=%fused_computation.2.clone | custom fusion | bytes 6291488 | tf_op jit(solution)/shard_map/jit(_take)/gather | solution.py:139
  86.6 3.9 select_multiply_fusion.1
  90.5 9.0 %all-to-all-done.3 = bf16[8,2,24,2048]{3,2,1,0:T(8,128)(2,1)} async-done(((bf16[8,2,24,2048]{3,2,1,0:T(8,128)(2,1)}), bf16[8,2,24,2048]{3,2,1,0:T(8,128)(2,1)}, u32[]{:S(2)}, u32[]{:S(2)}) %all-to-all-start.3) | async-done | bytes 1572896 | tf_op jit(solution)/shard_map/all_to_all | solution.py:153
  99.6 4.4 %all-to-all-start.2 = ((bf16[8,2,24,4096]{3,2,1,0:T(8,128)(2,1)}), bf16[8,2,24,4096]{3,2,1,0:T(8,128)(2,1)}, u32[]{:S(2)}, u32[]{:S(2)}) async-start(bf16[8,2,24,4096]{3,2,1,0:T(8,128)(2,1)} %select_multiply_fusion.1), calls=%async_computation.2 | async-start | bytes 6291456 | tf_op jit(solution)/shard_map/all_to_all | solution.py:156
  104.0 11.1 %gather_fusion.1 = bf16[192,8,2,512]{3,2,1,0:T(2,128)(2,1)} fusion(bf16[160,8,2,512]{3,2,1,0:T(2,128)(2,1)S(1)} %copy-done.5, s32[1024]{0:T(1024)S(1)} %pad_clamp_fusion.2), kind=kCustom, calls=%fused_computation.13 | custom fusion | bytes 6292224 | tf_op jit(solution)/shard_map/jit(_take)/gather | solution.py:122
  115.1 2.7 copy.81
  117.8 1.9 broadcast_select_fusion.2
  119.8 4.3 %gather_fusion.6 = bf16[8,24,8,2,512]{4,2,3,1,0:T(8,128)(2,1)} fusion(bf16[8,24,8,2,512]{4,2,3,1,0:T(8,128)(2,1)} %broadcast_select_fusion.2, s32[1024]{0:T(1024)S(1)} %pad_clamp_fusion.1), kind=kCustom, calls=%fused_computation.1.clone | custom fusion | bytes 6291488 | tf_op jit(solution)/shard_map/jit(_take)/gather | solution.py:139
  124.1 3.9 select_multiply_fusion.2
  128.1 46.1 %all-to-all-done.2 = bf16[8,2,24,4096]{3,2,1,0:T(8,128)(2,1)} async-done(((bf16[8,2,24,4096]{3,2,1,0:T(8,128)(2,1)}), bf16[8,2,24,4096]{3,2,1,0:T(8,128)(2,1)}, u32[]{:S(2)}, u32[]{:S(2)}) %all-to-all-start.2) | async-done | bytes 3145760 | tf_op jit(solution)/shard_map/all_to_all | solution.py:156
  174.2 4.4 %all-to-all-start.1 = ((bf16[8,24,8,2,512]{4,2,3,1,0:T(8,128)(2,1)}), bf16[8,24,8,2,512]{4,2,3,1,0:T(8,128)(2,1)}, u32[]{:S(2)}, u32[]{:S(2)}) async-start(bf16[8,24,8,2,512]{4,2,3,1,0:T(8,128)(2,1)} %select_multiply_fusion.2), calls=%async_computation.1 | async-start | bytes 6291456 | tf_op jit(solution)/shard_map/all_to_all | solution.py:159
  179.1 5.4 %gather_fusion.14 = bf16[8,2048,128]{2,1,0:T(8,128)(2,1)} fusion(bf16[8,2048,128]{2,1,0:T(8,128)(2,1)} %param.30, s32[1024]{0:T(1024)S(1)} %pad_clamp_fusion.1), kind=kCustom, calls=%fused_computation.5.clone | custom fusion | bytes 8388640 | tf_op jit(solution)/shard_map/jit(_take)/gather | solution.py:139
  184.6 4.7 %select_multiply_fusion = bf16[8,2048,128]{2,1,0:T(8,128)(2,1)} fusion(bf16[8,2048,128]{2,1,0:T(8,128)(2,1)} %gather_fusion.14, pred[8]{0:T(512)(128)(4,1)S(1)} %compare_and_fusion.2, bf16[8]{0:T(256)(128)(2,1)S(1)} %convert_element_type.70), kind=kLoop, calls=%fused_computation.25 | loop fusion | flops 4194304 | bytes 8388632 | tf_op jit(solution)/shard_map/mul | solution.py:141
  189.3 2.1 gather_fusion.11
  191.3 57.5 %all-to-all-done.1 = bf16[8,24,8,2,512]{4,2,3,1,0:T(8,128)(2,1)} async-done(((bf16[8,24,8,2,512]{4,2,3,1,0:T(8,128)(2,1)}), bf16[8,24,8,2,512]{4,2,3,1,0:T(8,128)(2,1)}, u32[]{:S(2)}, u32[]{:S(2)}) %all-to-all-start.1) | async-done | bytes 3145760 | tf_op jit(solution)/shard_map/all_to_all | solution.py:159
  248.8 4.6 %all-to-all-start.5 = ((bf16[8,2048,128]{2,1,0:T(8,128)(2,1)}), bf16[8,2048,128]{2,1,0:T(8,128)(2,1)}, u32[]{:S(2)}, u32[]{:S(2)}) async-start(bf16[8,2048,128]{2,1,0:T(8,128)(2,1)} %select_multiply_fusion), calls=%async_computation.6 | async-start | bytes 8388608 | tf_op jit(solution)/shard_map/all_to_all | solution.py:147
  253.9 4.6 %convolution_bitcast_fusion = f32[384,1,1024]{2,0,1:T(8,128)S(1)} fusion(bf16[384,2048]{1,0:T(8,128)(2,1)S(1)} %bitcast.114, bf16[2048,1024]{1,0:T(8,128)(2,1)} %param.29), kind=kOutput, calls=%fused_computation.52 | convolution fusion | flops 1610612736 | bytes 7340032 | tf_op jit(solution)/shard_map/dot_general | solution.py:21
  258.5 1.8 convolution_bitcast_fusion.1
  260.3 1.9 pad_maximum_fusion
  262.3 0.6 gather_fusion.5
  263.1 1.8 gather_fusion.13
  265.0 4.3 %gather_fusion.9 = bf16[8,2,24,4096]{3,2,1,0:T(8,128)(2,1)} fusion(bf16[8,2,24,4096]{3,2,1,0:T(8,128)(2,1)} %all-to-all-done.2, s32[1024]{0:T(1024)S(1)} %pad_clamp_fusion), kind=kCustom, calls=%fused_computation.8.clone | custom fusion | bytes 6291488 | tf_op jit(solution)/shard_map/jit(_take)/gather | solution.py:144
  269.3 2.7 broadcast_select_fusion
  272.0 2.5 copy.106
  274.6 4.3 %gather_fusion.7 = bf16[8,24,8,2,512]{4,2,3,1,0:T(8,128)(2,1)} fusion(bf16[8,24,8,2,512]{4,2,3,1,0:T(8,128)(2,1)} %all-to-all-done.1, s32[1024]{0:T(1024)S(1)} %pad_clamp_fusion), kind=kCustom, calls=%fused_computation.7.clone | custom fusion | bytes 6291488 | tf_op jit(solution)/shard_map/jit(_take)/gather | solution.py:144
  278.9 2.4 broadcast_select_fusion.1
  281.3 1.6 copy-done.3
  282.9 16.2 %bitcast_reduce_fusion = (f32[8,2,24,4,8]{4,1,3,2,0:T(2,128)S(1)}, f32[8,24,4,8,2,8]{5,3,4,2,1,0:T(8,128)}) fusion(pred[8,24,8]{2,1,0:T(8,128)(4,1)S(1)} %iota_compare_fusion.1, bf16[8,2,24,4,8,128]{5,4,3,2,1,0:T(8,128)(2,1)S(1)} %bitcast.106, bf16[8,24,8,2,512]{4,2,3,1,0:T(8,128)(2,1)S(1)} %broadcast_select_fusion.1), kind=kOutput, calls=%fused_computation.17 | convolution fusion | flops 25448448 | bytes 5185536 | tf_op jit(solution)/shard_map/stnghd,snpgd->stnghp/dot_general | solution.py:50
  299.1 46.9 %all-to-all-done.5 = bf16[8,2048,128]{2,1,0:T(8,128)(2,1)} async-done(((bf16[8,2048,128]{2,1,0:T(8,128)(2,1)}), bf16[8,2048,128]{2,1,0:T(8,128)(2,1)}, u32[]{:S(2)}, u32[]{:S(2)}) %all-to-all-start.5) | async-done | bytes 4194336 | tf_op jit(solution)/shard_map/all_to_all | solution.py:147
  345.9 5.3 %gather_fusion.15 = bf16[8,2048,128]{2,1,0:T(8,128)(2,1)} fusion(bf16[8,2048,128]{2,1,0:T(8,128)(2,1)} %all-to-all-done.5, s32[1024]{0:T(1024)S(1)} %pad_clamp_fusion), kind=kCustom, calls=%fused_computation.11.clone | custom fusion | bytes 8388640 | tf_op jit(solution)/shard_map/jit(_take)/gather | solution.py:144
  351.3 3.6 fusion.2
  354.9 4.2 %all-reduce.2 = bf16[8,48,128]{2,1,0:T(8,128)(2,1)S(1)} all-reduce(f32[8,48,128]{2,1,0:T(8,128)S(1)} %fusion.2), channel_id=1, replica_groups=mesh['grp'=2,'inst'=8,'tp'=2] {'tp'}, use_global_device_ids=true, to_apply=%region_12.19 | all-reduce | flops 49152 | bytes 294912 | tf_op jit(solution)/shard_map/psum | solution.py:30
  359.2 1.9 fusion.13
  361.3 1.7 copy.93
  363.0 0.9 reshape_squeeze.15
  364.0 16.4 %fusion.32 = (f32[8,2,24,4,8]{4,1,3,2,0:T(2,128)S(1)}, f32[8,2,24,4,8,2]{4,5,1,3,2,0:T(2,128)S(1)}) fusion(bf16[8,2,24,4,8,128]{5,4,3,2,1,0:T(8,128)(2,1)} %bitcast.105, bf16[8,2,24,4,128,1]{4,3,2,1,0,5:T(4,128)(2,1)S(1)} %bitcast.119, pred[2,2]{1,0:T(4,128)(4,1)S(1)} %iota_compare_fusion.6), kind=kOutput, calls=%fused_computation.108 | convolution fusion | flops 6352896 | bytes 3686404 | tf_op jit(solution)/shard_map/stnghd,sungd->stnghu/dot_general | solution.py:62
  380.8 3.3 fusion.18
  384.2 3.6 fusion.1
  388.3 2.6 fusion.6
  390.9 2.9 fusion.5
  393.8 2.3 copy.91
  396.1 5.8 %reshape.208 = bf16[8,2,24,4096]{3,2,1,0:T(8,128)(2,1)} reshape(bf16[8,2,24,4,8,128]{5,4,3,2,1,0:T(8,128)(2,1)} %copy.91) | data formatting | bytes 6291456 | tf_op jit(solution)/shard_map/reshape | solution.py:86
  402.0 4.1 copy.92
  (66 shorter events, 3.5 us)
Async XLA Ops:
  7.2 56.3 %copy-start = (bf16[2,160,4096]{2,1,0:T(8,128)(2,1)S(1)}, bf16[2,160,4096]{2,1,0:T(8,128)(2,1)}, u32[]{:S(2)}) copy-start(bf16[2,160,4096]{2,1,0:T(8,128)(2,1)} %param.23) | copy-start | bytes 7864324
  14.9 13.7 %all-to-all-start = ((bf16[8,1,24]{2,1,0:T(2,128)(2,1)}), bf16[8,1,24]{2,1,0:T(2,128)(2,1)S(1)}, u32[]{:S(2)}, u32[]{:S(2)}) async-start(bf16[8,1,24]{2,1,0:T(2,128)(2,1)} %copy.80), calls=%async_computation | async-start | bytes 8192 | tf_op jit(solution)/shard_map/all_to_all | solution.py:162
  28.6 30.3 %all-to-all-start.4 = ((bf16[8,2,64,512]{3,2,1,0:T(8,128)(2,1)}), bf16[8,2,64,512]{3,2,1,0:T(8,128)(2,1)}, u32[]{:S(2)}, u32[]{:S(2)}) async-start(bf16[8,2,64,512]{3,2,1,0:T(8,128)(2,1)} %select_multiply_fusion.4), calls=%async_computation.5 | async-start | bytes 2097152 | tf_op jit(solution)/shard_map/all_to_all | solution.py:150
  58.9 40.7 %all-to-all-start.3 = ((bf16[8,2,24,2048]{3,2,1,0:T(8,128)(2,1)}), bf16[8,2,24,2048]{3,2,1,0:T(8,128)(2,1)}, u32[]{:S(2)}, u32[]{:S(2)}) async-start(bf16[8,2,24,2048]{3,2,1,0:T(8,128)(2,1)} %select_multiply_fusion.3), calls=%async_computation.3 | async-start | bytes 3145728 | tf_op jit(solution)/shard_map/all_to_all | solution.py:153
  90.5 13.5 %copy-start.5 = (bf16[160,8,2,512]{3,2,1,0:T(2,128)(2,1)S(1)}, bf16[160,8,2,512]{3,2,1,0:T(2,128)(2,1)}, u32[]{:S(2)}) copy-start(bf16[160,8,2,512]{3,2,1,0:T(2,128)(2,1)} %param.24) | copy-start | bytes 7864324
  99.6 74.6 %all-to-all-start.2 = ((bf16[8,2,24,4096]{3,2,1,0:T(8,128)(2,1)}), bf16[8,2,24,4096]{3,2,1,0:T(8,128)(2,1)}, u32[]{:S(2)}, u32[]{:S(2)}) async-start(bf16[8,2,24,4096]{3,2,1,0:T(8,128)(2,1)} %select_multiply_fusion.1), calls=%async_computation.2 | async-start | bytes 6291456 | tf_op jit(solution)/shard_map/all_to_all | solution.py:156
  128.1 50.6 %copy-start.9 = (s32[64]{0:T(128)S(1)}, s32[64]{0:T(128)}, u32[]{:S(2)}) copy-start(s32[64]{0:T(128)} %param.27) | copy-start | bytes 772
  174.2 74.6 %all-to-all-start.1 = ((bf16[8,24,8,2,512]{4,2,3,1,0:T(8,128)(2,1)}), bf16[8,24,8,2,512]{4,2,3,1,0:T(8,128)(2,1)}, u32[]{:S(2)}, u32[]{:S(2)}) async-start(bf16[8,24,8,2,512]{4,2,3,1,0:T(8,128)(2,1)} %select_multiply_fusion.2), calls=%async_computation.1 | async-start | bytes 6291456 | tf_op jit(solution)/shard_map/all_to_all | solution.py:159
  248.8 97.1 %all-to-all-start.5 = ((bf16[8,2048,128]{2,1,0:T(8,128)(2,1)}), bf16[8,2048,128]{2,1,0:T(8,128)(2,1)}, u32[]{:S(2)}, u32[]{:S(2)}) async-start(bf16[8,2048,128]{2,1,0:T(8,128)(2,1)} %select_multiply_fusion), calls=%async_computation.6 | async-start | bytes 8388608 | tf_op jit(solution)/shard_map/all_to_all | solution.py:147
  253.4 105.8 %reduce-scatter.2.cloned.1.call-start = ((), (), s32[]{:S(2)}) async-start(), calls=%async_computation.7 | async-start | bytes 4718592 | tf_op jit(solution)/shard_map/reduce_scatter | solution.py:29
  253.8 4.6 %copy-start.6 = (bf16[8,2,24,2048]{3,2,1,0:T(8,128)(2,1)}, bf16[8,2,24,2048]{3,2,1,0:T(8,128)(2,1)S(1)}, u32[]{:S(2)}) copy-start(bf16[8,2,24,2048]{3,2,1,0:T(8,128)(2,1)S(1)} %broadcast_select_fusion.3) | copy-start | bytes 4718596
  253.9 4.6 %copy-start.8 = (bf16[2048,1024]{1,0:T(8,128)(2,1)S(1)}, bf16[2048,1024]{1,0:T(8,128)(2,1)}, u32[]{:S(2)}) copy-start(bf16[2048,1024]{1,0:T(8,128)(2,1)} %param.28) | copy-start | bytes 12582916
  278.9 4.0 copy-start.2
  281.3 1.6 copy-start.3
  363.9 20.2 %slice-start = ((s8[6291456]{0:T(1024)(128)(4,1)}), s8[4194304]{0:T(1024)(128)(4,1)S(1)}, s32[]{:S(2)}) async-start(s8[6291456]{0:T(1024)(128)(4,1)} %bitcast.101), calls=%async_computation.8 | async-start | bytes 8388608
  363.9 20.2 %slice-start.1 = ((s8[6291456]{0:T(1024)(128)(4,1)}), s8[2097152]{0:T(1024)(128)(4,1)S(1)}, s32[]{:S(2)}) async-start(s8[6291456]{0:T(1024)(128)(4,1)} %bitcast.101), calls=%async_computation.9 | async-start | bytes 4194304
  384.2 4.1 copy-start.4
  388.3 2.6 copy-start.7
  402.0 4.1 copy-start.1
Sparse Core Ops, SparseCore 0:
  262.4 12.1 reduce-scatter.1
where the time goes:
time: 420 us; the launch traced here: 413 us
  waiting for transfers between devices  166 us (40%)
  local copies, waits for them, and re-layouts  103 us (25%)
  matrix products  50 us (12%)
  other arithmetic  45.4 us (11%)
  starting transfers between devices  30.3 us (7%)
  between operations  14.9 us (4%)
    all_to_all x1, waiting for transfers between devices, on_device(): lax.all_to_all(outgoing_adapters(seg_cache), 'inst', split_axis=0, concat...  57.5 us
    all_to_all x1, waiting for transfers between devices, on_device(): lax.all_to_all(outgoing_adapters(adapter_down_maps), 'inst', split_axis=0...  46.9 us
    all_to_all x1, waiting for transfers between devices, on_device(): lax.all_to_all(outgoing_adapters(seg_queries), 'inst', split_axis=0, conc...  46.1 us
    gather x6, local copies, waits for them, and re-layouts, outgoing_adapters(): selected = jnp.take(payload, picked_slot, axis=0)  20.6 us
    gather x6, local copies, waits for them, and re-layouts, inward(): return jnp.take(payload, anchor, axis=0)  18.4 us
    mul x5, other arithmetic, outgoing_adapters(): return selected * retain  17.7 us
    dot_general x1, matrix products, project_slots(): jnp.einsum('stnghd,sungd->stnghu', query_head_rows, appended_keys, prefer...  16.4 us
    dot_general x1, matrix products, project_slots(): jnp.einsum('stnghd,snpgd->stnghp', query_head_rows, previous_keys, prefer...  16.2 us
  transfers between devices with their start and end apart: 7, of which 6 were waited for; matrix products, arithmetic and copies ran while one was open for 34% of the time, Pallas kernels for 0%

commit v1 on v0

v1 whole, which is shorter than its diff:
```python
import functools

import jax
import jax.numpy as jnp
from jax import lax
from jax.experimental import pallas as pl
from jax.experimental.pallas import tpu as pltpu
from jax.sharding import PartitionSpec as P

QUERY_GROUP = 8
HEAD_SIZE = 128
SEG = 24
NB = 16
LANE = 16
VMEM_LIMIT = 48 * 1024 * 1024


def project_kernel(
    part_ref, tok_ref, key_ref, value_ref, down_ref, idx_ref,
    other_key, other_value, mine_key, mine_value, low_ref,
):
    j = pl.program_id(0)
    half = pl.num_programs(0) // 2
    tok = tok_ref[...]
    key_part = jnp.dot(tok, key_ref[...], preferred_element_type=jnp.float32)
    value_part = jnp.dot(tok, value_ref[...], preferred_element_type=jnp.float32)

    @pl.when(j < half)
    def _():
        other_key[...] = key_part
        other_value[...] = value_part

    @pl.when(j >= half)
    def _():
        mine_key[...] = key_part
        mine_value[...] = value_part

    each = down_ref.shape[0]
    total = jnp.where(j == 0, 0.0, low_ref[...])
    for a in range(each):
        low = jnp.dot(tok, down_ref[a], preferred_element_type=jnp.float32)
        total = jnp.where(idx_ref[...] == j * each + a, low, total)
    low_ref[...] = total


def project(tokens, key_matrix, value_matrix, down, idx):
    rows, depth = tokens.shape
    slots, _, rank = down.shape
    width = key_matrix.shape[1]
    steps = 4
    tile = width // steps
    per = slots // steps
    half = steps // 2
    part = lax.axis_index("tp").astype(jnp.int32).reshape(1)

    def columns(j, part_ref):
        return (0, lax.rem((1 - part_ref[0]) * half + j, steps))

    other = pl.BlockSpec((rows, tile), lambda j, p: (0, jnp.minimum(j, half - 1)))
    mine = pl.BlockSpec((rows, tile), lambda j, p: (0, jnp.maximum(j - half, 0)))
    out = jax.ShapeDtypeStruct((rows, width // 2), jnp.float32)
    return pl.pallas_call(
        project_kernel,
        grid_spec=pltpu.PrefetchScalarGridSpec(
            num_scalar_prefetch=1,
            grid=(steps,),
            in_specs=[
                pl.BlockSpec((rows, depth), lambda j, p: (0, 0)),
                pl.BlockSpec((depth, tile), columns),
                pl.BlockSpec((depth, tile), columns),
                pl.BlockSpec((per, depth, rank), lambda j, p: (j, 0, 0)),
                pl.BlockSpec((rows, 1), lambda j, p: (0, 0)),
            ],
            out_specs=[other, other, mine, mine, pl.BlockSpec((rows, rank), lambda j, p: (0, 0))],
        ),
        out_shape=[out, out, out, out, jax.ShapeDtypeStruct((rows, rank), jnp.float32)],
        compiler_params=pltpu.CompilerParams(vmem_limit_bytes=VMEM_LIMIT),
        cost_estimate=pl.CostEstimate(
            flops=2 * rows * depth * (2 * width + slots * rank),
            bytes_accessed=2 * depth * (rows + 2 * width + slots * rank) + 8 * rows * width,
            transcendentals=0,
        ),
        name="project",
    )(part, tokens, key_matrix, value_matrix, down, idx)


def fold_matrix(rows, n_of, p_base, lane_base):
    r = lax.broadcasted_iota(jnp.int32, (rows, 128), 0)
    c = lax.broadcasted_iota(jnp.int32, (rows, 128), 1)
    return (c == lane_base + p_base + r // n_of).astype(jnp.bfloat16)


def weights_kernel(
    steps_t, requests,
    q_ref, k_ref, valid_ref, mk_ref, mv_ref, rk_ref, rv_ref, ml_ref, rl_ref, idx_ref, up_ref,
    fresh_ref, wts_ref,
):
    b = pl.program_id(0)
    width = mk_ref.shape[1]
    heads = width // HEAD_SIZE
    context = k_ref.shape[1] // width

    @pl.when(b == 0)
    def _():
        low = (ml_ref[...] + rl_ref[...]).astype(jnp.bfloat16)
        rank = low.shape[1] // 2
        idx = idx_ref[...]
        key = mk_ref[...] + rk_ref[...]
        value = mv_ref[...] + rv_ref[...]
        for s in range(up_ref.shape[0]):
            part = jnp.where(idx == s, low, jnp.zeros_like(low))
            key += jnp.dot(part[:, :rank], up_ref[s, 0], preferred_element_type=jnp.float32)
            value += jnp.dot(part[:, rank:], up_ref[s, 1], preferred_element_type=jnp.float32)
        fresh_ref[:, :width] = key.astype(jnp.bfloat16)
        fresh_ref[:, width:] = value.astype(jnp.bfloat16)

    rows = QUERY_GROUP * steps_t * NB
    old_lanes = context * NB
    new_lanes = steps_t * NB
    row = lax.broadcasted_iota(jnp.int32, (rows, old_lanes), 0)
    lane = lax.broadcasted_iota(jnp.int32, (rows, old_lanes), 1)
    old_ok = (row % NB == lane % NB) & (valid_ref[0] > 0)
    row = lax.broadcasted_iota(jnp.int32, (rows, new_lanes), 0)
    lane = lax.broadcasted_iota(jnp.int32, (rows, new_lanes), 1)
    new_ok = (row % NB == lane % NB) & (lane // NB <= (row // NB) % steps_t)
    factor = HEAD_SIZE ** (-0.5)
    q = q_ref[...].reshape(steps_t * NB, q_ref.shape[-1])
    k = k_ref[...]
    new_k = [fresh_ref[pl.ds(t * requests + b * NB, NB), :width] for t in range(steps_t)]
    new_k = jnp.concatenate(new_k, axis=0)
    half = rows // 2
    total = jnp.zeros((half, 128), jnp.float32)
    dims = (((1,), (1,)), ((), ()))
    for g in range(heads):
        here = slice(g * HEAD_SIZE, (g + 1) * HEAD_SIZE)
        start = g * QUERY_GROUP * HEAD_SIZE
        qg = jnp.concatenate(
            [q[:, start + h * HEAD_SIZE : start + (h + 1) * HEAD_SIZE] for h in range(QUERY_GROUP)],
            axis=0,
        )
        kg = jnp.concatenate(
            [k[:, p * width + g * HEAD_SIZE : p * width + (g + 1) * HEAD_SIZE] for p in range(context)],
            axis=0,
        )
        old = lax.dot_general(qg, kg, dims, preferred_element_type=jnp.float32) * factor
        new = lax.dot_general(qg, new_k[:, here], dims, preferred_element_type=jnp.float32) * factor
        old = jnp.where(old_ok, old, -jnp.inf)
        new = jnp.where(new_ok, new, -jnp.inf)
        top = jnp.maximum(
            jnp.max(old, axis=1, keepdims=True), jnp.max(new, axis=1, keepdims=True)
        )
        old = jnp.exp(old - top)
        new = jnp.exp(new - top)
        norm = jnp.sum(old, axis=1, keepdims=True) + jnp.sum(new, axis=1, keepdims=True)
        scale = 1.0 / norm
        old = (old * scale).astype(jnp.bfloat16)
        new = (new * scale).astype(jnp.bfloat16)
        for part in range(2):
            base = part * 64 + g * LANE
            span = slice(part * half, (part + 1) * half)
            total += jnp.dot(
                old[span], fold_matrix(old_lanes, NB, 0, base), preferred_element_type=jnp.float32
            )
            total += jnp.dot(
                new[span], fold_matrix(new_lanes, NB, context, base),
                preferred_element_type=jnp.float32,
            )
    total = total.astype(jnp.bfloat16)
    for i in range(half // NB):
        wts_ref[:, i * 128 : (i + 1) * 128] = total[i * NB : (i + 1) * NB]


def weigh(queries, keys, valid, mine, received, low_mine, low_received, idx, up):
    steps_t, requests, query_width = queries.shape
    rows, width = mine[0].shape
    blocks = requests // NB
    context = keys.shape[1] // width
    whole = lambda a: pl.BlockSpec(a.shape, lambda b: (0,) * a.ndim)
    packed = QUERY_GROUP * steps_t // 2 * 128
    return pl.pallas_call(
        functools.partial(weights_kernel, steps_t, requests),
        grid=(blocks,),
        in_specs=[
            pl.BlockSpec((steps_t, NB, query_width), lambda b: (0, b, 0)),
            pl.BlockSpec((NB, keys.shape[1]), lambda b: (b, 0)),
            pl.BlockSpec((1, 1, context * NB), lambda b: (b, 0, 0)),
        ]
        + [whole(a) for a in (*mine, *received, low_mine, low_received, idx, up)],
        out_specs=[
            pl.BlockSpec((rows, 2 * width), lambda b: (0, 0)),
            pl.BlockSpec((NB, packed), lambda b: (b, 0)),
        ],
        out_shape=[
            jax.ShapeDtypeStruct((rows, 2 * width), jnp.bfloat16),
            jax.ShapeDtypeStruct((requests, packed), jnp.bfloat16),
        ],
        compiler_params=pltpu.CompilerParams(vmem_limit_bytes=VMEM_LIMIT),
        cost_estimate=pl.CostEstimate(
            flops=10 ** 10, bytes_accessed=2 * 10 ** 7, transcendentals=10 ** 6
        ),
        name="weigh",
    )(queries, keys, valid, *mine, *received, low_mine, low_received, idx, up)


def serve_kernel(steps_t, width, v_ref, f_ref, w_ref, out_ref):
    heads = width // HEAD_SIZE
    context = v_ref.shape[1] // width
    rows = QUERY_GROUP * steps_t * NB
    half = rows // 2
    lanes = (context + steps_t) * NB
    row = lax.broadcasted_iota(jnp.int32, (rows, lanes), 0)
    lane = lax.broadcasted_iota(jnp.int32, (rows, lanes), 1)
    own = row % NB == lane % NB
    w = w_ref[...]
    w = jnp.concatenate([w[:, i * 128 : (i + 1) * 128] for i in range(half // NB)], axis=0)
    r = lax.broadcasted_iota(jnp.int32, (128, lanes), 0)
    c = lax.broadcasted_iota(jnp.int32, (128, lanes), 1)
    v = v_ref[...]
    fresh = f_ref[...]
    for g in range(heads):
        vg = [v[:, p * width + g * HEAD_SIZE : p * width + (g + 1) * HEAD_SIZE] for p in range(context)]
        for t in range(steps_t):
            start = (2 * t + 1) * width + g * HEAD_SIZE
            vg.append(fresh[:, start : start + HEAD_SIZE])
        vg = jnp.concatenate(vg, axis=0)
        wide = []
        for part in range(2):
            spread = (r == part * 64 + g * LANE + c // NB).astype(jnp.bfloat16)
            wide.append(jnp.dot(w, spread, preferred_element_type=jnp.float32))
        wide = jnp.concatenate(wide, axis=0)
        wide = jnp.where(own, wide, 0.0).astype(jnp.bfloat16)
        res = jnp.dot(wide, vg, preferred_element_type=jnp.float32).astype(jnp.bfloat16)
        for h in range(QUERY_GROUP):
            start = (g * QUERY_GROUP + h) * HEAD_SIZE
            out_ref[:, :, start : start + HEAD_SIZE] = res[
                h * steps_t * NB : (h + 1) * steps_t * NB
            ].reshape(steps_t, NB, HEAD_SIZE)


def serve(values, second, steps_t, width):
    rows = values.shape[0]
    query_width = width * QUERY_GROUP
    fresh_width = steps_t * 2 * width
    packed = second.shape[1] - fresh_width
    return pl.pallas_call(
        functools.partial(serve_kernel, steps_t, width),
        grid=(rows // NB,),
        in_specs=[
            pl.BlockSpec((NB, values.shape[1]), lambda b: (b, 0)),
            pl.BlockSpec((NB, fresh_width), lambda b: (b, 0)),
            pl.BlockSpec((NB, packed), lambda b: (b, fresh_width // packed)),
        ],
        out_specs=pl.BlockSpec((steps_t, NB, query_width), lambda b: (0, b, 0)),
        out_shape=jax.ShapeDtypeStruct((steps_t, rows, query_width), jnp.bfloat16),
        compiler_params=pltpu.CompilerParams(vmem_limit_bytes=VMEM_LIMIT),
        cost_estimate=pl.CostEstimate(
            flops=10 ** 10, bytes_accessed=10 ** 7, transcendentals=0
        ),
        name="serve",
    )(values, second, second)


def on_device(
    tokens,
    queries,
    key_value_cache,
    key_value_length,
    request_adapter_index,
    adapter_destination,
    key_matrix,
    value_matrix,
    adapter_down_maps,
    adapter_up_maps,
):
    slot_count = adapter_down_maps.shape[0]
    requests = request_adapter_index.shape[0]
    steps_t = tokens.shape[0]
    context = key_value_cache.shape[1]
    width = key_value_cache.shape[3]
    instances = lax.axis_size("inst")
    own_index = lax.axis_index("inst")
    chosen = request_adapter_index[:, 0]
    order = jnp.arange(requests)
    same = (chosen[:, None] == chosen[None, :]) & (order[:, None] > order[None, :])
    within = jnp.sum(same.astype(jnp.int32), axis=1)
    leaving = lax.dynamic_slice_in_dim(adapter_destination, own_index * slot_count, slot_count)
    towards = jnp.sum(
        jnp.where(chosen[:, None] == jnp.arange(slot_count)[None, :], leaving[None, :], 0), axis=1
    )
    seat = towards * SEG + within
    pick = (seat[None, :] == jnp.arange(instances * SEG)[:, None]).astype(jnp.bfloat16)

    def move(rows):
        sent = jnp.dot(pick, rows, preferred_element_type=jnp.float32).astype(jnp.bfloat16)
        sent = sent.reshape(instances, SEG, rows.shape[1])
        got = lax.all_to_all(sent, "inst", split_axis=0, concat_axis=0, tiled=True)
        if instances != slot_count:
            coming = jnp.sum(
                (adapter_destination.reshape(instances, slot_count) == own_index).astype(jnp.int32),
                axis=1,
            )
            rank = jnp.cumsum(coming) - 1
            hit = coming[None, :] * (rank[None, :] == jnp.arange(slot_count)[:, None])
            anchor = jnp.sum(hit * jnp.arange(instances)[None, :], axis=1)
            got = jnp.take(got, anchor, axis=0)
        return got.reshape(slot_count * SEG, rows.shape[1])

    values = move(key_value_cache[:, :, 1].reshape(requests, context * width))
    keys = key_value_cache[:, :, 0].reshape(requests, context * width)
    idx = jnp.tile(chosen, steps_t)[:, None]
    other_key, other_value, mine_key, mine_value, low = project(
        tokens.reshape(steps_t * requests, -1), key_matrix, value_matrix, adapter_down_maps, idx
    )
    swap = lambda a: lax.ppermute(a, "tp", [(0, 1), (1, 0)])
    valid = (jnp.arange(context)[None, :, None] < key_value_length.reshape(-1, 1, NB)).astype(
        jnp.int32
    )
    fresh, weights = weigh(
        queries,
        keys,
        valid.reshape(-1, 1, context * NB),
        (mine_key, mine_value),
        (swap(other_key), swap(other_value)),
        low,
        swap(low),
        idx,
        adapter_up_maps,
    )
    second = jnp.concatenate([fresh[t * requests : (t + 1) * requests] for t in range(steps_t)] + [weights], axis=1)
    second = move(second)
    attended = serve(values, second, steps_t, width)
    new_kv = second[:, : steps_t * 2 * width].reshape(-1, steps_t, 2, width)
    return (attended, jnp.swapaxes(new_kv, 0, 1))


def solution(mesh):
    return jax.shard_map(
        on_device,
        mesh=mesh,
        in_specs=(
            P(None, ("grp", "inst"), "tp"),
            P(None, ("grp", "inst"), "tp"),
            P(("grp", "inst"), None, None, "tp"),
            P(("grp", "inst")),
            P(("grp", "inst"), None),
            P("grp"),
            P("tp", None),
            P("tp", None),
            P(("grp", "inst"), "tp", None),
            P(("grp", "inst"), None, None, "tp"),
        ),
        out_specs=(P(None, ("grp", "inst"), "tp"), P(None, ("grp", "inst"), None, "tp")),
        check_vma=False,
    )
```

time: 420 us -> 134 us (0.32); the launches traced: 413 us -> 133 us
  waiting for transfers between devices: 166 us -> 59.2 us
  local copies, waits for them, and re-layouts: 103 us -> 27.5 us
  matrix products: 50 us -> 3.21 us
  other arithmetic: 45.4 us -> 0.28 us
  Pallas kernels: 0 us -> 30.4 us
  starting transfers between devices: 30.3 us -> 11.7 us
  between operations: 14.9 us -> 0.79 us
    all_to_all x6 -> x2, waiting for transfers between devices: 166 us -> 59.2 us  [move(): got = lax.all_to_all(sent, 'inst', split_axis=0, concat_axis=0, tiled=True)]
    gather x18 -> x0, local copies, waits for them, and re-layouts: 81.7 us -> none  [the longest x6 20.6 us: outgoing_adapters(): selected = jnp.take(payload, picked_slot, axis=0)]
    dot_general x8 -> x2, matrix products: 50 us -> 3.21 us  [move(): jnp.dot(pick, rows, preferred_element_type=jnp.float32).astype(jnp.bfloat16)]
    pallas_call x0 -> x3, Pallas kernels: none -> 30.4 us  [the longest x1 12.4 us: weigh(): pl.pallas_call(functools.partial(weights_kernel, steps_t, requests), grid...]
    all_to_all x6 -> x2, starting transfers between devices: 30 us -> 10.7 us  [move(): got = lax.all_to_all(sent, 'inst', split_axis=0, concat_axis=0, tiled=True)]
    mul x5 -> x0, other arithmetic: 17.7 us -> none  [outgoing_adapters(): return selected * retain]
    slice x1 -> x3, local copies, waits for them, and re-layouts: 0.21 us -> 15 us  [the longest x1 14 us: on_device(): keys = key_value_cache[:, :, 0].reshape(requests, context * width)]
    reduce_sum x7 -> x2, other arithmetic: 8.19 us -> 0.27 us  [the longest x1 0.19 us: on_device(): within = jnp.sum(same.astype(jnp.int32), axis=1)]
  transfers between devices with their start and end apart: 7 -> 5, of which waited for: 6 -> 2; matrix products, arithmetic and copies ran while one was open for 34% -> 18% of each run, Pallas kernels for 0% -> 0%
where the time goes in v1:
time: 134 us; the launch traced here: 133 us
  waiting for transfers between devices  59.2 us (44%)
  Pallas kernels  30.4 us (23%)
  local copies, waits for them, and re-layouts  27.5 us (21%)
  starting transfers between devices  11.7 us (9%)
  matrix products  3.21 us (2%)
    all_to_all x2, waiting for transfers between devices, move(): got = lax.all_to_all(sent, 'inst', split_axis=0, concat_axis=0, tiled=True)  59.2 us
    slice x1, local copies, waits for them, and re-layouts, on_device(): keys = key_value_cache[:, :, 0].reshape(requests, context * width)  14 us
    pallas_call x1, Pallas kernels, weigh(): pl.pallas_call(functools.partial(weights_kernel, steps_t, requests), grid...  12.4 us
    all_to_all x2, starting transfers between devices, move(): got = lax.all_to_all(sent, 'inst', split_axis=0, concat_axis=0, tiled=True)  10.7 us
    pallas_call x1, Pallas kernels, project(): pl.pallas_call(project_kernel, grid_spec=pltpu.PrefetchScalarGridSpec(num...  9.35 us
    pallas_call x1, Pallas kernels, serve(): pl.pallas_call(functools.partial(serve_kernel, steps_t, width), grid=(row...  8.66 us
    unnamed x22, local copies, waits for them, and re-layouts  7.3 us
    reshape x2, local copies, waits for them, and re-layouts, on_device(): new_kv = second[:, :steps_t * 2 * width].reshape(-1, steps_t, 2, width)  3.97 us
  transfers between devices with their start and end apart: 5, of which 2 were waited for; matrix products, arithmetic and copies ran while one was open for 18% of the time, Pallas kernels for 0%

profile of v1, /device:TPU:0, one launch (start us, length us, event | category | flops | bytes accessed | tf_op | source)
XLA Modules:
  0.0 133.1 jit_solution(4544685999498992559)
XLA Ops:
  0.6 0.7 tile.2
  1.3 0.2 broadcast_in_dim_tile.4.idx_ref
  1.5 0.0 copy-start
  1.5 1.3 copy-done
  2.8 0.0 copy-start.8
  2.8 9.4 %project.1 = (f32[320,512]{1,0:T(8,128)S(1)}, f32[320,512]{1,0:T(8,128)S(1)}, f32[320,512]{1,0:T(8,128)S(1)}, f32[320,512]{1,0:T(8,128)S(1)}, f32[320,128]{1,0:T(8,128)S(1)}) custom-call(s32[1]{0:T(128)} %bitcast.3.part_ref, bf16[320,2048]{1,0:T(8,128)(2,1)S(1)} %bitcast.19, bf16[2048,1024]{1,0:T(8,128)(2,1)} %key_ref.1, bf16[2048,1024]{1,0:T(8,128)(2,1)} %value_ref.1, ...), custom_call_target="tpu_custom_call" | custom-call | flops 4026531840 | bytes 16515072 | tf_op jit(solution)/shard_map/project/pallas_call | solution.py:62
  12.2 0.0 copy-start.2
  12.2 0.8 copy-done.2
  13.0 0.0 copy-start.4
  13.0 0.9 copy-done.4
  13.9 0.4 collective-permute-start.2
  14.4 0.1 collective-permute-start
  14.4 0.4 collective-permute-start.1
  14.9 0.1 lt.33
  15.0 0.0 copy-done.8
  15.0 0.1 lt.35
  15.0 0.1 lt.37
  15.1 14.0 %slice_reduce_fusion = (bf16[160,8,512]{2,1,0:T(8,128)(2,1)S(1)}, bf16[160,8,512]{2,1,0:T(8,128)(2,1)}) fusion(bf16[160,8,2,512]{3,2,1,0:T(2,128)(2,1)} %param.12), kind=kLoop, calls=%fused_computation.2 | loop fusion | bytes 5242880 | tf_op jit(solution)/shard_map/slice | solution.py:309
  29.2 0.0 copy-start.9
  29.2 0.0 copy-start.7
  29.2 0.0 copy-start.1
  29.2 1.6 %copy.20 = bf16[20,8,8,512]{3,1,2,0:T(8,128)(2,1)} copy(bf16[20,8,8,512]{3,2,1,0:T(8,128)(2,1)S(1)} %bitcast.23) | data formatting | bytes 2621440
  30.8 0.0 copy-done.9
  30.8 0.1 dynamic_slice.3
  30.9 0.0 copy-done.7
  30.9 0.1 select_reduce_fusion
  31.0 0.2 convert_reduce_fusion
  31.2 0.0 collective-permute-done.2.rl_ref
  31.2 0.0 collective-permute-done.rk_ref
  31.2 0.0 collective-permute-done.1.rv_ref
  31.2 0.0 copy-done.1
  31.2 0.0 copy-start.3
  31.2 1.1 copy-done.3
  32.3 0.0 copy-start.5
  32.3 1.1 copy-done.5
  33.4 12.4 %weigh.1 = (bf16[320,1024]{1,0:T(8,128)(2,1)S(1)}, bf16[160,1024]{1,0:T(8,128)(2,1)S(1)}) custom-call(bf16[2,160,4096]{2,1,0:T(8,128)(2,1)} %q_ref.1, bf16[160,4096]{1,0:T(8,128)(2,1)} %bitcast.24, s32[10,1,128]{2,1,0:T(1,128)S(1)} %compare_convert_fusion.valid_ref, f32[320,512]{1,0:T(8,128)S(1)} %copy-done.3, f32[320,512]{1,0:T(8,128)S(1)} %copy-done.5, ...), custom_call_target="tpu_custom_call" | custom-call | flops 10000000000 | bytes 20000000 | tf_op jit(solution)/shard_map/weigh/pallas_call | solution.py:180
  45.9 1.5 %convolution_convert_fusion.1 = bf16[192,3072]{1,0:T(8,128)(2,1)} fusion(bf16[160,1024]{1,0:T(8,128)(2,1)S(1)} %get-tuple-element.15, bf16[160,1024]{1,0:T(8,128)(2,1)S(1)} %get-tuple-element.19, bf16[160,1024]{1,0:T(8,128)(2,1)S(1)} %get-tuple-element.18, s32[160]{0:T(256)S(1)} %multiply_add_fusion), kind=kOutput, calls=%fused_computation.1 | convolution fusion | flops 192313344 | bytes 2163328 | tf_op jit(solution)/shard_map/dot_general | solution.py:294
  47.4 0.0 copy-start.6
  47.4 7.0 %all-to-all-start.1 = ((bf16[8,24,3072]{2,1,0:T(8,128)(2,1)}), bf16[8,24,3072]{2,1,0:T(8,128)(2,1)S(1)}, u32[]{:S(2)}, u32[]{:S(2)}) async-start(bf16[8,24,3072]{2,1,0:T(8,128)(2,1)} %bitcast.25), calls=%async_computation.1 | async-start | bytes 2359296 | tf_op jit(solution)/shard_map/all_to_all | solution.py:296
  54.3 0.0 copy-done.6
  54.3 0.5 copy.19
  54.9 1.7 %convolution_convert_fusion = bf16[192,4096]{1,0:T(8,128)(2,1)} fusion(bf16[160,4096]{1,0:T(8,128)(2,1)S(1)} %bitcast.21, s32[160]{0:T(256)S(1)} %multiply_add_fusion), kind=kOutput, calls=%fused_computation | convolution fusion | flops 252475392 | bytes 2884224 | tf_op jit(solution)/shard_map/dot_general | solution.py:294
  56.6 27.0 %all-to-all-done.1 = bf16[8,24,3072]{2,1,0:T(8,128)(2,1)S(1)} async-done(((bf16[8,24,3072]{2,1,0:T(8,128)(2,1)}), bf16[8,24,3072]{2,1,0:T(8,128)(2,1)S(1)}, u32[]{:S(2)}, u32[]{:S(2)}) %all-to-all-start.1) | async-done | bytes 1179680 | tf_op jit(solution)/shard_map/all_to_all | solution.py:296
  83.6 3.8 %all-to-all-start = ((bf16[8,24,4096]{2,1,0:T(8,128)(2,1)}), bf16[8,24,4096]{2,1,0:T(8,128)(2,1)S(1)}, u32[]{:S(2)}, u32[]{:S(2)}) async-start(bf16[8,24,4096]{2,1,0:T(8,128)(2,1)} %bitcast.20), calls=%async_computation | async-start | bytes 3145728 | tf_op jit(solution)/shard_map/all_to_all | solution.py:296
  87.3 0.9 slice.20
  88.3 2.6 %reshape.79 = bf16[192,2,2,512]{3,2,1,0:T(2,128)(2,1)S(1)} reshape(bf16[192,2048]{1,0:T(8,128)(2,1)} %slice.20) | data formatting | bytes 1572864 | tf_op jit(solution)/shard_map/reshape | solution.py:332
  90.9 1.4 %copy.22 = bf16[192,2,2,512]{3,2,0,1:T(2,128)(2,1)} copy(bf16[192,2,2,512]{3,2,1,0:T(2,128)(2,1)S(1)} %reshape.79) | data formatting | bytes 1572864 | tf_op jit(solution)/shard_map/reshape | solution.py:332
  92.3 32.2 %all-to-all-done = bf16[8,24,4096]{2,1,0:T(8,128)(2,1)S(1)} async-done(((bf16[8,24,4096]{2,1,0:T(8,128)(2,1)}), bf16[8,24,4096]{2,1,0:T(8,128)(2,1)S(1)}, u32[]{:S(2)}, u32[]{:S(2)}) %all-to-all-start) | async-done | bytes 1572896 | tf_op jit(solution)/shard_map/all_to_all | solution.py:296
  124.5 8.7 %serve.1 = bf16[2,192,4096]{2,1,0:T(8,128)(2,1)} custom-call(bf16[192,4096]{1,0:T(8,128)(2,1)S(1)} %bitcast.18, bf16[192,3072]{1,0:T(8,128)(2,1)S(1)} %bitcast.16, bf16[192,3072]{1,0:T(8,128)(2,1)S(1)} %bitcast.17), custom_call_target="tpu_custom_call" | custom-call | flops 10000000000 | bytes 10000000 | tf_op jit(solution)/shard_map/serve/pallas_call | solution.py:245
  (5 shorter events, 0.1 us)
Async XLA Ops:
  1.5 1.3 copy-start
  2.8 12.1 %copy-start.8 = (s32[160]{0:T(256)S(1)}, s32[160]{0:T(256)}, u32[]{:S(2)}) copy-start(s32[160]{0:T(256)} %param.13) | copy-start | bytes 1924
  12.2 0.8 copy-start.2
  13.0 0.9 copy-start.4
  13.9 17.3 %collective-permute-start.2 = (f32[320,128]{1,0:T(8,128)S(1)}, f32[320,128]{1,0:T(8,128)S(1)}, u32[]{:S(2)}, u32[]{:S(2)}) collective-permute-start(f32[320,128]{1,0:T(8,128)S(1)} %get-tuple-element.13.ml_ref), channel_id=1, source_target_pairs={{0,1},{1,0},{2,3},{3,2},{4,5},{5,4},{6,7},{7,6},{8,9},{9,8},{10,11... | collective-permute-start | bytes 491528 | tf_op jit(solution)/shard_map/ppermute | solution.py:314
  14.4 16.8 %collective-permute-start = (f32[320,512]{1,0:T(8,128)S(1)}, f32[320,512]{1,0:T(8,128)S(1)}, u32[]{:S(2)}, u32[]{:S(2)}) collective-permute-start(f32[320,512]{1,0:T(8,128)S(1)} %get-tuple-element.11), channel_id=1, source_target_pairs={{0,1},{1,0},{2,3},{3,2},{4,5},{5,4},{6,7},{7,6},{8,9},{9,8},{10,11... | collective-permute-start | bytes 1966088 | tf_op jit(solution)/shard_map/ppermute | solution.py:314
  14.4 16.8 %collective-permute-start.1 = (f32[320,512]{1,0:T(8,128)S(1)}, f32[320,512]{1,0:T(8,128)}, u32[]{:S(2)}, u32[]{:S(2)}) collective-permute-start(f32[320,512]{1,0:T(8,128)S(1)} %get-tuple-element.12), channel_id=1, source_target_pairs={{0,1},{1,0},{2,3},{3,2},{4,5},{5,4},{6,7},{7,6},{8,9},{9,8},{10,11... | collective-permute-start | bytes 1966088 | tf_op jit(solution)/shard_map/ppermute | solution.py:314
  29.2 1.6 %copy-start.9 = (s32[64]{0:T(128)S(1)}, s32[64]{0:T(128)}, u32[]{:S(2)}) copy-start(s32[64]{0:T(128)} %param.15) | copy-start | bytes 772
  29.2 1.7 %copy-start.7 = (s32[160,1]{0,1:T(1,128)S(1)}, s32[160,1]{0,1:T(1,128)}, u32[]{:S(2)}) copy-start(s32[160,1]{0,1:T(1,128)} %param.14) | copy-start | bytes 1924
  29.2 2.0 %copy-start.1 = (bf16[8,2,64,512]{3,2,1,0:T(8,128)(2,1)S(1)}, bf16[8,2,64,512]{3,2,1,0:T(8,128)(2,1)}, u32[]{:S(2)}) copy-start(bf16[8,2,64,512]{3,2,1,0:T(8,128)(2,1)} %up_ref.1) | copy-start | bytes 3145732
  31.2 1.1 copy-start.3
  32.3 1.1 copy-start.5
  47.4 7.0 %copy-start.6 = (bf16[160,8,512]{2,1,0:T(8,128)(2,1)S(1)}, bf16[160,8,512]{2,1,0:T(8,128)(2,1)}, u32[]{:S(2)}) copy-start(bf16[160,8,512]{2,1,0:T(8,128)(2,1)} %get-tuple-element.17) | copy-start | bytes 3932164
  47.4 36.2 %all-to-all-start.1 = ((bf16[8,24,3072]{2,1,0:T(8,128)(2,1)}), bf16[8,24,3072]{2,1,0:T(8,128)(2,1)S(1)}, u32[]{:S(2)}, u32[]{:S(2)}) async-start(bf16[8,24,3072]{2,1,0:T(8,128)(2,1)} %bitcast.25), calls=%async_computation.1 | async-start | bytes 2359296 | tf_op jit(solution)/shard_map/all_to_all | solution.py:296
  83.6 40.9 %all-to-all-start = ((bf16[8,24,4096]{2,1,0:T(8,128)(2,1)}), bf16[8,24,4096]{2,1,0:T(8,128)(2,1)S(1)}, u32[]{:S(2)}, u32[]{:S(2)}) async-start(bf16[8,24,4096]{2,1,0:T(8,128)(2,1)} %bitcast.20), calls=%async_computation | async-start | bytes 3145728 | tf_op jit(solution)/shard_map/all_to_all | solution.py:296

commit v2 on v1

--- a/solution.py
+++ b/solution.py
@@ -82,6 +82,64 @@
         ),
         name="project",
     )(part, tokens, key_matrix, value_matrix, down, idx)
+
+
+def split_kernel(leaving_ref, row_ref, col_ref, cache_ref, sent_ref, keys_ref, pick_ref, vals):
+    requests = col_ref.shape[0]
+    width = cache_ref.shape[1]
+    context = keys_ref.shape[1] // width
+    block = 2 * context * NB
+    chosen = row_ref[...]
+    r = lax.broadcasted_iota(jnp.int32, (requests, requests), 0)
+    c = lax.broadcasted_iota(jnp.int32, (requests, requests), 1)
+    same = jnp.where((col_ref[...] == chosen) & (r < c), 1, 0)
+    seat = jnp.sum(same, axis=0, keepdims=True)
+    for a in range(leaving_ref.shape[0]):
+        seat += jnp.where(chosen == a, leaving_ref[a] * SEG, 0)
+    slots = pick_ref.shape[0]
+    pick = lax.broadcasted_iota(jnp.int32, (slots, requests), 0) == seat
+    pick = pick.astype(jnp.bfloat16)
+    pick_ref[...] = pick
+    r = lax.broadcasted_iota(jnp.int32, (block // 2, block), 0)
+    c = lax.broadcasted_iota(jnp.int32, (block // 2, block), 1)
+    first = (r % NB) * (2 * context) + (r // NB) * 2
+    take_key = (c == first).astype(jnp.bfloat16)
+    take_value = (c == first + 1).astype(jnp.bfloat16)
+    for b in range(requests // NB):
+        x = cache_ref[b * block : (b + 1) * block]
+        k = jnp.dot(take_key, x, preferred_element_type=jnp.float32).astype(jnp.bfloat16)
+        v = jnp.dot(take_value, x, preferred_element_type=jnp.float32).astype(jnp.bfloat16)
+        here = slice(b * NB, (b + 1) * NB)
+        for p in range(context):
+            lanes = slice(p * width, (p + 1) * width)
+            keys_ref[here, lanes] = k[p * NB : (p + 1) * NB]
+            vals[here, lanes] = v[p * NB : (p + 1) * NB]
+    for p in range(context):
+        lanes = slice(p * width, (p + 1) * width)
+        moved = jnp.dot(pick, vals[:, lanes], preferred_element_type=jnp.float32)
+        sent_ref[:, lanes] = moved.astype(jnp.bfloat16)
+
+
+def split(cache, chosen, leaving, slots):
+    requests, context, _, width = cache.shape
+    vmem = pl.BlockSpec(memory_space=pltpu.VMEM)
+    wide = context * width
+    return pl.pallas_call(
+        split_kernel,
+        in_specs=[pl.BlockSpec(memory_space=pltpu.SMEM), vmem, vmem, vmem],
+        out_specs=[vmem, vmem, vmem],
+        out_shape=[
+            jax.ShapeDtypeStruct((slots, wide), jnp.bfloat16),
+            jax.ShapeDtypeStruct((requests, wide), jnp.bfloat16),
+            jax.ShapeDtypeStruct((slots, requests), jnp.bfloat16),
+        ],
+        scratch_shapes=[pltpu.VMEM((requests, wide), jnp.bfloat16)],
+        compiler_params=pltpu.CompilerParams(vmem_limit_bytes=VMEM_LIMIT),
+        cost_estimate=pl.CostEstimate(
+            flops=10 ** 9, bytes_accessed=2 * (slots + 3 * requests) * wide, transcendentals=0
+        ),
+        name="split",
+    )(leaving, chosen[None, :], chosen[:, None], cache.reshape(-1, width))
 
 
 def fold_matrix(rows, n_of, p_base, lane_base):
@@ -202,7 +260,7 @@
     )(queries, keys, valid, *mine, *received, low_mine, low_received, idx, up)
 
 
-def serve_kernel(steps_t, width, v_ref, f_ref, w_ref, out_ref):
+def serve_kernel(steps_t, width, v_ref, f_ref, w_ref, out_ref, kv_ref):
     heads = width // HEAD_SIZE
     context = v_ref.shape[1] // width
     rows = QUERY_GROUP * steps_t * NB
@@ -217,6 +275,15 @@
     c = lax.broadcasted_iota(jnp.int32, (128, lanes), 1)
     v = v_ref[...]
     fresh = f_ref[...]
+    r2 = lax.broadcasted_iota(jnp.int32, (2 * NB, 2 * NB), 0)
+    c2 = lax.broadcasted_iota(jnp.int32, (2 * NB, 2 * NB), 1)
+    weave = (c2 == (r2 % 2) * NB + r2 // 2).astype(jnp.bfloat16)
+    for t in range(steps_t):
+        pair = [fresh[:, (2 * t + i) * width : (2 * t + i + 1) * width] for i in range(2)]
+        pair = jnp.dot(
+            weave, jnp.concatenate(pair, axis=0), preferred_element_type=jnp.float32
+        )
+        kv_ref[t] = pair.reshape(NB, 2, width).astype(jnp.bfloat16)
     for g in range(heads):
         vg = [v[:, p * width + g * HEAD_SIZE : p * width + (g + 1) * HEAD_SIZE] for p in range(context)]
         for t in range(steps_t):
@@ -250,8 +317,14 @@
             pl.BlockSpec((NB, fresh_width), lambda b: (b, 0)),
             pl.BlockSpec((NB, packed), lambda b: (b, fresh_width // packed)),
         ],
-        out_specs=pl.BlockSpec((steps_t, NB, query_width), lambda b: (0, b, 0)),
-        out_shape=jax.ShapeDtypeStruct((steps_t, rows, query_width), jnp.bfloat16),
+        out_specs=[
+            pl.BlockSpec((steps_t, NB, query_width), lambda b: (0, b, 0)),
+            pl.BlockSpec((steps_t, NB, 2, width), lambda b: (0, b, 0, 0)),
+        ],
+        out_shape=[
+            jax.ShapeDtypeStruct((steps_t, rows, query_width), jnp.bfloat16),
+            jax.ShapeDtypeStruct((steps_t, rows, 2, width), jnp.bfloat16),
+        ],
         compiler_params=pltpu.CompilerParams(vmem_limit_bytes=VMEM_LIMIT),
         cost_estimate=pl.CostEstimate(
             flops=10 ** 10, bytes_accessed=10 ** 7, transcendentals=0
@@ -280,19 +353,11 @@
     instances = lax.axis_size("inst")
     own_index = lax.axis_index("inst")
     chosen = request_adapter_index[:, 0]
-    order = jnp.arange(requests)
-    same = (chosen[:, None] == chosen[None, :]) & (order[:, None] > order[None, :])
-    within = jnp.sum(same.astype(jnp.int32), axis=1)
     leaving = lax.dynamic_slice_in_dim(adapter_destination, own_index * slot_count, slot_count)
-    towards = jnp.sum(
-        jnp.where(chosen[:, None] == jnp.arange(slot_count)[None, :], leaving[None, :], 0), axis=1
-    )
-    seat = towards * SEG + within
-    pick = (seat[None, :] == jnp.arange(instances * SEG)[:, None]).astype(jnp.bfloat16)
-
-    def move(rows):
-        sent = jnp.dot(pick, rows, preferred_element_type=jnp.float32).astype(jnp.bfloat16)
-        sent = sent.reshape(instances, SEG, rows.shape[1])
+    sent, keys, pick = split(key_value_cache, chosen, leaving, instances * SEG)
+
+    def move(sent):
+        sent = sent.reshape(instances, SEG, sent.shape[1])
         got = lax.all_to_all(sent, "inst", split_axis=0, concat_axis=0, tiled=True)
         if instances != slot_count:
             coming = jnp.sum(
@@ -303,11 +368,11 @@
             hit = coming[None, :] * (rank[None, :] == jnp.arange(slot_count)[:, None])
             anchor = jnp.sum(hit * jnp.arange(instances)[None, :], axis=1)
             got = jnp.take(got, anchor, axis=0)
-        return got.reshape(slot_count * SEG, rows.shape[1])
-
-    values = move(key_value_cache[:, :, 1].reshape(requests, context * width))
-    keys = key_value_cache[:, :, 0].reshape(requests, context * width)
+        return got.reshape(slot_count * SEG, sent.shape[2])
+
     idx = jnp.tile(chosen, steps_t)[:, None]
+    sent, idx = lax.optimization_barrier((sent, idx))
+    values = move(sent)
     other_key, other_value, mine_key, mine_value, low = project(
         tokens.reshape(steps_t * requests, -1), key_matrix, value_matrix, adapter_down_maps, idx
     )
@@ -327,10 +392,10 @@
         adapter_up_maps,
     )
     second = jnp.concatenate([fresh[t * requests : (t + 1) * requests] for t in range(steps_t)] + [weights], axis=1)
+    second = jnp.dot(pick, second, preferred_element_type=jnp.float32).astype(jnp.bfloat16)
+    second, values = lax.optimization_barrier((second, values))
     second = move(second)
-    attended = serve(values, second, steps_t, width)
-    new_kv = second[:, : steps_t * 2 * width].reshape(-1, steps_t, 2, width)
-    return (attended, jnp.swapaxes(new_kv, 0, 1))
+    return serve(values, second, steps_t, width)
 
 
 def solution(mesh):

time: 134 us -> 96.8 us (0.72)
  waiting for transfers between devices: 59.2 us -> 8.42 us
  blocking collectives: 0 us -> 32.5 us
  local copies, waits for them, and re-layouts: 27.5 us -> 13.2 us
  starting transfers between devices: 11.7 us -> 7.79 us
  matrix products: 3.21 us -> 0.46 us
  Pallas kernels: 30.4 us -> 33.1 us
    all_to_all x2 -> x1, waiting for transfers between devices: 59.2 us -> 5.74 us  [move(): got = lax.all_to_all(sent, 'inst', split_axis=0, concat_axis=0, tiled=True)]
    all_to_all x0 -> x1, blocking collectives: none -> 32.5 us  [move(): got = lax.all_to_all(sent, 'inst', split_axis=0, concat_axis=0, tiled=True)]
    slice x2 -> x0, local copies, waits for them, and re-layouts: 15 us -> none  [the longest x1 14 us: on_device(): keys = key_value_cache[:, :, 0].reshape(requests, context * width)]
    all_to_all x2 -> x1, starting transfers between devices: 10.7 us -> 7.28 us  [move(): got = lax.all_to_all(sent, 'inst', split_axis=0, concat_axis=0, tiled=True)]
    dot_general x2 -> x1, matrix products: 3.21 us -> 0.46 us  [on_device(): jnp.dot(pick, second, preferred_element_type=jnp.float32)]
    ppermute x3, waiting for transfers between devices: 0.01 us -> 2.68 us  [on_device(): swap = lambda a: lax.ppermute(a, 'tp', [(0, 1), (1, 0)])]
    pallas_call x0 -> x1, Pallas kernels: none -> 1.92 us  [split(): pl.pallas_call(split_kernel, in_specs=[pl.BlockSpec(memory_space=pltpu.SM...]
    unnamed x22 -> x23, local copies, waits for them, and re-layouts: 7.3 us -> 8.1 us
  transfers between devices with their start and end apart: 5 -> 4, of which waited for: 2 -> 3; matrix products, arithmetic and copies ran while one was open for 18% -> 1% of each run, Pallas kernels for 0% -> 23%
where the time goes in v2:
time: 96.8 us; the launch traced here: 96.2 us
  Pallas kernels  33.1 us (34%)
  blocking collectives  32.5 us (34%)
  local copies, waits for them, and re-layouts  13.2 us (14%)
  waiting for transfers between devices  8.42 us (9%)
  starting transfers between devices  7.79 us (8%)
    all_to_all x1, blocking collectives, move(): got = lax.all_to_all(sent, 'inst', split_axis=0, concat_axis=0, tiled=True)  32.5 us
    pallas_call x1, Pallas kernels, weigh(): pl.pallas_call(functools.partial(weights_kernel, steps_t, requests), grid...  12.1 us
    pallas_call x1, Pallas kernels, project(): pl.pallas_call(project_kernel, grid_spec=pltpu.PrefetchScalarGridSpec(num...  9.87 us
    pallas_call x1, Pallas kernels, serve(): pl.pallas_call(functools.partial(serve_kernel, steps_t, width), grid=(row...  9.16 us
    unnamed x23, local copies, waits for them, and re-layouts  8.1 us
    all_to_all x1, starting transfers between devices, move(): got = lax.all_to_all(sent, 'inst', split_axis=0, concat_axis=0, tiled=True)  7.28 us
    all_to_all x1, waiting for transfers between devices, move(): got = lax.all_to_all(sent, 'inst', split_axis=0, concat_axis=0, tiled=True)  5.74 us
    reshape x1, local copies, waits for them, and re-layouts, split(): cache.reshape(-1, width)  3.78 us
  transfers between devices with their start and end apart: 4, of which 3 were waited for; matrix products, arithmetic and copies ran while one was open for 1% of the time, Pallas kernels for 23%

profile of v2, /device:TPU:0, one launch (start us, length us, event | category | flops | bytes accessed | tf_op | source)
XLA Modules:
  0.0 96.2 jit_solution(12812388895411242269)
XLA Ops:
  0.6 0.8 copy.13.col_ref
  1.4 0.7 tile.8
  2.1 0.1 broadcast_in_dim_tile.3
  2.2 0.0 copy-start.10
  2.2 0.0 copy-start.1
  2.2 3.8 %reshape.66.cache_ref = bf16[2560,512]{1,0:T(8,128)(2,1)S(1)} reshape(bf16[160,8,2,512]{3,2,1,0:T(2,128)(2,1)} %param.12) | data formatting | bytes 5242880 | tf_op jit(solution)/shard_map/reshape | solution.py:142
  6.0 0.0 copy-done.10
  6.0 0.1 dynamic_slice.3.leaving_ref
  6.1 0.0 copy-done.1
  6.1 1.9 %split.1 = (bf16[192,4096]{1,0:T(8,128)(2,1)S(1)}, bf16[160,4096]{1,0:T(8,128)(2,1)S(1)}, bf16[192,160]{1,0:T(8,128)(2,1)S(1)}) custom-call(s32[8]{0:T(128)S(1)} %dynamic_slice.3.leaving_ref, s32[1,160]{1,0:T(1,128)S(1)} %bitcast.14, s32[160,1]{1,0:T(8,128)S(1)} %copy.13.col_ref, bf16[2560,512]{1,0:T(8,128)(2,1)S(1)} %reshape.66.cache_ref), custom_call_target="tpu_custom_call" | custom-call | flops 1000000000 | bytes 5505024 | tf_op jit(solution)/shard_map/split/pallas_call | solution.py:127
  8.0 0.0 copy-start.4
  8.0 1.1 %copy-done.4 = bf16[160,4096]{1,0:T(8,128)(2,1)} copy-done((bf16[160,4096]{1,0:T(8,128)(2,1)}, bf16[160,4096]{1,0:T(8,128)(2,1)S(1)}, u32[]{:S(2)}) %copy-start.4) | copy-done | bytes 1310744
  9.1 0.0 copy-start
  9.1 0.0 copy-start.2
  9.1 1.1 %copy-done = bf16[192,4096]{1,0:T(8,128)(2,1)} copy-done((bf16[192,4096]{1,0:T(8,128)(2,1)}, bf16[192,4096]{1,0:T(8,128)(2,1)S(1)}, u32[]{:S(2)}) %copy-start) | copy-done | bytes 1572888
  10.2 7.3 %all-to-all-start = ((bf16[8,24,4096]{2,1,0:T(8,128)(2,1)}), bf16[8,24,4096]{2,1,0:T(8,128)(2,1)S(1)}, u32[]{:S(2)}, u32[]{:S(2)}) async-start(bf16[8,24,4096]{2,1,0:T(8,128)(2,1)} %bitcast.10), calls=%async_computation | async-start | bytes 3145728 | tf_op jit(solution)/shard_map/all_to_all | solution.py:361
  17.5 0.1 copy.14.idx_ref
  17.7 0.0 copy-done.2
  17.7 0.0 copy-start.9
  17.7 9.9 %project.1 = (f32[320,512]{1,0:T(8,128)}, f32[320,512]{1,0:T(8,128)}, f32[320,512]{1,0:T(8,128)S(1)}, f32[320,512]{1,0:T(8,128)S(1)}, f32[320,128]{1,0:T(8,128)S(1)}) custom-call(s32[1]{0:T(128)} %bitcast.1.part_ref, bf16[320,2048]{1,0:T(8,128)(2,1)S(1)} %bitcast.15, bf16[2048,1024]{1,0:T(8,128)(2,1)} %key_ref.1, bf16[2048,1024]{1,0:T(8,128)(2,1)} %value_ref.1, ...), custom_call_target="tpu_custom_call" | custom-call | flops 4026531840 | bytes 16515072 | tf_op jit(solution)/shard_map/project/pallas_call | solution.py:62
  27.6 0.0 copy-start.5
  27.6 0.8 copy-done.5
  28.4 0.0 copy-start.7
  28.4 0.8 copy-done.7
  29.2 0.0 collective-permute-start
  29.2 0.5 collective-permute-start.1
  29.8 0.0 collective-permute-start.2
  29.8 0.1 lt.33
  29.8 0.0 copy-done.9
  29.8 0.1 lt.35
  29.9 0.1 lt.37
  30.0 1.8 %collective-permute-done.2.rl_ref = f32[320,128]{1,0:T(8,128)S(1)} collective-permute-done((f32[320,128]{1,0:T(8,128)S(1)}, f32[320,128]{1,0:T(8,128)S(1)}, u32[]{:S(2)}, u32[]{:S(2)}) %collective-permute-start.2) | collective-permute-done | bytes 163872 | tf_op jit(solution)/shard_map/ppermute | solution.py:379
  31.8 0.0 collective-permute-done.rk_ref
  31.8 0.9 collective-permute-done.1.rv_ref
  32.7 0.0 copy-start.3
  32.7 1.2 %copy-done.3 = bf16[8,2,64,512]{3,2,1,0:T(8,128)(2,1)S(1)} copy-done((bf16[8,2,64,512]{3,2,1,0:T(8,128)(2,1)S(1)}, bf16[8,2,64,512]{3,2,1,0:T(8,128)(2,1)}, u32[]{:S(2)}) %copy-start.3) | copy-done | bytes 1048600
  33.9 0.0 copy-start.6
  33.9 1.1 %copy-done.6 = f32[320,512]{1,0:T(8,128)S(1)} copy-done((f32[320,512]{1,0:T(8,128)S(1)}, f32[320,512]{1,0:T(8,128)}, u32[]{:S(2)}) %copy-start.6) | copy-done | bytes 655384
  35.0 0.0 copy-start.8
  35.0 1.1 %copy-done.8 = f32[320,512]{1,0:T(8,128)S(1)} copy-done((f32[320,512]{1,0:T(8,128)S(1)}, f32[320,512]{1,0:T(8,128)}, u32[]{:S(2)}) %copy-start.8) | copy-done | bytes 655384
  36.1 12.1 %weigh.1 = (bf16[320,1024]{1,0:T(8,128)(2,1)S(1)}, bf16[160,1024]{1,0:T(8,128)(2,1)S(1)}) custom-call(bf16[2,160,4096]{2,1,0:T(8,128)(2,1)} %q_ref.1, bf16[160,4096]{1,0:T(8,128)(2,1)} %copy-done.4, s32[10,1,128]{2,1,0:T(1,128)S(1)} %compare_convert_fusion.valid_ref, f32[320,512]{1,0:T(8,128)S(1)} %copy-done.6, f32[320,512]{1,0:T(8,128)S(1)} %copy-done.8, ...), custom_call_target="tpu_custom_call" | custom-call | flops 10000000000 | bytes 20000000 | tf_op jit(solution)/shard_map/weigh/pallas_call | solution.py:238
  48.3 0.5 convolution_convert_fusion
  48.8 5.7 %all-to-all-done = bf16[8,24,4096]{2,1,0:T(8,128)(2,1)S(1)} async-done(((bf16[8,24,4096]{2,1,0:T(8,128)(2,1)}), bf16[8,24,4096]{2,1,0:T(8,128)(2,1)S(1)}, u32[]{:S(2)}, u32[]{:S(2)}) %all-to-all-start) | async-done | bytes 1572896 | tf_op jit(solution)/shard_map/all_to_all | solution.py:361
  54.5 32.5 %all_to_all.10 = bf16[8,24,3072]{2,1,0:T(8,128)(2,1)S(1)} all-to-all(bf16[8,24,3072]{2,1,0:T(8,128)(2,1)S(1)} %bitcast.16), channel_id=1, replica_groups=mesh['grp'=2,'inst'=8,'tp'=2] {'inst'}, dimensions={0} | all-to-all | bytes 2359296 | tf_op jit(solution)/shard_map/all_to_all | solution.py:361
  87.0 9.2 %serve.1 = (bf16[2,192,4096]{2,1,0:T(8,128)(2,1)}, bf16[2,192,2,512]{3,2,1,0:T(2,128)(2,1)}) custom-call(bf16[192,4096]{1,0:T(8,128)(2,1)S(1)} %bitcast.9, bf16[192,3072]{1,0:T(8,128)(2,1)S(1)} %bitcast.11, bf16[192,3072]{1,0:T(8,128)(2,1)S(1)} %bitcast.12), custom_call_target="tpu_custom_call" | custom-call | flops 10000000000 | bytes 10000000 | tf_op jit(solution)/shard_map/serve/pallas_call | solution.py:312
  (4 shorter events, 0.1 us)
Async XLA Ops:
  2.2 3.8 %copy-start.10 = (s32[64]{0:T(128)S(1)}, s32[64]{0:T(128)}, u32[]{:S(2)}) copy-start(s32[64]{0:T(128)} %param.15) | copy-start | bytes 772
  2.2 3.9 %copy-start.1 = (s32[160,1]{0,1:T(1,128)S(1)}, s32[160,1]{0,1:T(1,128)}, u32[]{:S(2)}) copy-start(s32[160,1]{0,1:T(1,128)} %param.14) | copy-start | bytes 1924
  8.0 1.1 %copy-start.4 = (bf16[160,4096]{1,0:T(8,128)(2,1)}, bf16[160,4096]{1,0:T(8,128)(2,1)S(1)}, u32[]{:S(2)}) copy-start(bf16[160,4096]{1,0:T(8,128)(2,1)S(1)} %get-tuple-element.17.k_ref) | copy-start | bytes 3932164
  9.1 1.1 %copy-start = (bf16[192,4096]{1,0:T(8,128)(2,1)}, bf16[192,4096]{1,0:T(8,128)(2,1)S(1)}, u32[]{:S(2)}) copy-start(bf16[192,4096]{1,0:T(8,128)(2,1)S(1)} %get-tuple-element.27) | copy-start | bytes 4718596
  9.1 8.6 %copy-start.2 = (bf16[2,160,2048]{2,1,0:T(8,128)(2,1)S(1)}, bf16[2,160,2048]{2,1,0:T(8,128)(2,1)}, u32[]{:S(2)}) copy-start(bf16[2,160,2048]{2,1,0:T(8,128)(2,1)} %param.10) | copy-start | bytes 3932164
  10.2 44.3 %all-to-all-start = ((bf16[8,24,4096]{2,1,0:T(8,128)(2,1)}), bf16[8,24,4096]{2,1,0:T(8,128)(2,1)S(1)}, u32[]{:S(2)}, u32[]{:S(2)}) async-start(bf16[8,24,4096]{2,1,0:T(8,128)(2,1)} %bitcast.10), calls=%async_computation | async-start | bytes 3145728 | tf_op jit(solution)/shard_map/all_to_all | solution.py:361
  17.7 12.2 %copy-start.9 = (s32[160]{0:T(256)S(1)}, s32[160]{0:T(256)}, u32[]{:S(2)}) copy-start(s32[160]{0:T(256)} %param.13) | copy-start | bytes 1924
  27.6 0.8 copy-start.5
  28.4 0.8 copy-start.7
  29.2 2.6 %collective-permute-start = (f32[320,512]{1,0:T(8,128)}, f32[320,512]{1,0:T(8,128)S(1)}, u32[]{:S(2)}, u32[]{:S(2)}) collective-permute-start(f32[320,512]{1,0:T(8,128)} %get-tuple-element.22), channel_id=1, source_target_pairs={{0,1},{1,0},{2,3},{3,2},{4,5},{5,4},{6,7},{7,6},{8,9},{9,8},{10,11... | collective-permute-start | bytes 1966088 | tf_op jit(solution)/shard_map/ppermute | solution.py:379
  29.2 3.5 %collective-permute-start.1 = (f32[320,512]{1,0:T(8,128)}, f32[320,512]{1,0:T(8,128)S(1)}, u32[]{:S(2)}, u32[]{:S(2)}) collective-permute-start(f32[320,512]{1,0:T(8,128)} %get-tuple-element.23), channel_id=1, source_target_pairs={{0,1},{1,0},{2,3},{3,2},{4,5},{5,4},{6,7},{7,6},{8,9},{9,8},{10,11... | collective-permute-start | bytes 1966088 | tf_op jit(solution)/shard_map/ppermute | solution.py:379
  29.8 2.1 %collective-permute-start.2 = (f32[320,128]{1,0:T(8,128)S(1)}, f32[320,128]{1,0:T(8,128)S(1)}, u32[]{:S(2)}, u32[]{:S(2)}) collective-permute-start(f32[320,128]{1,0:T(8,128)S(1)} %get-tuple-element.24.ml_ref), channel_id=1, source_target_pairs={{0,1},{1,0},{2,3},{3,2},{4,5},{5,4},{6,7},{7,6},{8,9},{9,8},{10,11... | collective-permute-start | bytes 491528 | tf_op jit(solution)/shard_map/ppermute | solution.py:379
  32.7 1.2 %copy-start.3 = (bf16[8,2,64,512]{3,2,1,0:T(8,128)(2,1)S(1)}, bf16[8,2,64,512]{3,2,1,0:T(8,128)(2,1)}, u32[]{:S(2)}) copy-start(bf16[8,2,64,512]{3,2,1,0:T(8,128)(2,1)} %up_ref.1) | copy-start | bytes 3145732
  33.9 1.1 %copy-start.6 = (f32[320,512]{1,0:T(8,128)S(1)}, f32[320,512]{1,0:T(8,128)}, u32[]{:S(2)}) copy-start(f32[320,512]{1,0:T(8,128)} %copy-done.5) | copy-start | bytes 1966084
  35.0 1.1 %copy-start.8 = (f32[320,512]{1,0:T(8,128)S(1)}, f32[320,512]{1,0:T(8,128)}, u32[]{:S(2)}) copy-start(f32[320,512]{1,0:T(8,128)} %copy-done.7) | copy-start | bytes 1966084

commit v3 on v0

v3 whole, which is shorter than its diff:
```python
import functools

import jax
import jax.numpy as jnp
from jax import lax
from jax.experimental import pallas as pl
from jax.experimental.pallas import tpu as pltpu
from jax.sharding import PartitionSpec as P

QUERY_GROUP = 8
HEAD_SIZE = 128
SEG = 24
NB = 16
LANE = 16
PIECES = 4
VMEM_LIMIT = 56 * 1024 * 1024
F32 = jnp.float32
BF16 = jnp.bfloat16


def dot(a, b):
    return jnp.dot(a, b, preferred_element_type=F32)


def iota(shape, axis):
    return lax.broadcasted_iota(jnp.int32, shape, axis)


def fold_matrix(rows, n_of, p_base, lane_base):
    return (iota((rows, 128), 1) == lane_base + p_base + iota((rows, 128), 0) // n_of).astype(BF16)


def kernel(
    n, steps_t,
    leaving_ref, row_ref, col_ref, idx_ref, valid_ref,
    cache_hbm, tok_hbm, key_hbm, value_hbm, down_hbm, up_hbm, query_hbm,
    out_ref, kv_ref,
    cache, tok, key, value, down, up, query,
    pick_ref, vals, keys, sent_v, got_v, sent_s, got_s,
    part_k, part_v, got_k, got_vv, low_ref, got_low, fresh, wts,
    load_sem, piece_sem, pair_send, pair_recv, send_sem, recv_sem,
):
    me = lax.axis_index("inst")
    core = lax.axis_index("tp")
    requests = col_ref.shape[0]
    width = cache.shape[1]
    context = vals.shape[1] // width
    heads = width // HEAD_SIZE
    slots = down.shape[0]
    tile = key.shape[2]

    loads = [
        pltpu.make_async_copy(src, dst, load_sem.at[i])
        for i, (src, dst) in enumerate(
            [(cache_hbm, cache), (tok_hbm, tok), (down_hbm, down), (up_hbm, up), (query_hbm, query)]
        )
    ]
    pieces = []
    for j in range(PIECES):
        col = lax.rem((1 - core) * (PIECES // 2) + j, PIECES) * tile
        col = pl.multiple_of(col, tile)
        for i, (src, dst) in enumerate([(key_hbm, key), (value_hbm, value)]):
            pieces.append(
                pltpu.make_async_copy(src.at[:, pl.ds(col, tile)], dst.at[j], piece_sem.at[i, j])
            )
    loads[0].start()
    loads[1].start()
    for piece in pieces:
        piece.start()
    for load in loads[2:]:
        load.start()

    barrier = pltpu.get_barrier_semaphore()
    for k in range(1, n):
        pl.semaphore_signal(
            barrier, inc=1, device_id={"inst": lax.rem(me + k, n)},
            device_id_type=pl.DeviceIdType.MESH,
        )
    pl.semaphore_signal(
        barrier, inc=1, device_id={"tp": 1 - core}, device_id_type=pl.DeviceIdType.MESH
    )

    chosen = row_ref[...]
    r = iota((requests, requests), 0)
    c = iota((requests, requests), 1)
    same = jnp.where((col_ref[...] == chosen) & (r < c), 1, 0)
    seat = jnp.sum(same, axis=0, keepdims=True)
    for a in range(slots):
        seat += jnp.where(chosen == a, leaving_ref[a] * SEG, 0)
    pick_ref[...] = (iota((n * SEG, requests), 0) == seat).astype(BF16)

    block = 2 * context * NB
    r = iota((block // 2, block), 0)
    c = iota((block // 2, block), 1)
    first = (r % NB) * (2 * context) + (r // NB) * 2
    take_key = (c == first).astype(BF16)
    take_value = (c == first + 1).astype(BF16)
    loads[0].wait()

    def split(take, into):
        def body(b, carry):
            x = cache[pl.ds(pl.multiple_of(b * block, block), block)]
            v = dot(take, x).astype(BF16)
            here = pl.ds(pl.multiple_of(b * NB, NB), NB)
            for p in range(context):
                into[here, p * width : (p + 1) * width] = v[p * NB : (p + 1) * NB]
            return carry

        lax.fori_loop(0, requests // NB, body, 0)

    split(take_value, vals)
    pick = pick_ref[...]

    def place(rows, into, lanes):
        moved = dot(pick, rows)
        for d in range(n):
            into[d, :, lanes] = moved[d * SEG : (d + 1) * SEG].astype(BF16)

    for p in range(context):
        lanes = slice(p * width, (p + 1) * width)
        place(vals[:, lanes], sent_v, lanes)
    pl.semaphore_wait(barrier, n)

    def outgoing(i, k):
        src, dst = [(sent_v, got_v), (sent_s, got_s)][i]
        to = lax.rem(me + k, n)
        return pltpu.make_async_remote_copy(
            src_ref=src.at[to],
            dst_ref=dst.at[me],
            send_sem=send_sem.at[i, k],
            recv_sem=recv_sem.at[i, k],
            device_id={"inst": to},
            device_id_type=pl.DeviceIdType.MESH,
        )

    def incoming(i, k):
        src, dst = [(sent_v, got_v), (sent_s, got_s)][i]
        source = lax.rem(me - k + n, n)
        return pltpu.make_async_remote_copy(
            src_ref=src.at[source],
            dst_ref=dst.at[source],
            send_sem=send_sem.at[i, k],
            recv_sem=recv_sem.at[i, k],
            device_id={"inst": source},
            device_id_type=pl.DeviceIdType.MESH,
        )

    for k in range(1, n):
        outgoing(0, k).start()
    split(take_key, keys)

    loads[1].wait()

    def pair(i):
        src, dst = [(part_k.at[0 : PIECES // 2], got_k), (part_v.at[0 : PIECES // 2], got_vv), (low_ref, got_low)][i]
        return pltpu.make_async_remote_copy(
            src_ref=src,
            dst_ref=dst,
            send_sem=pair_send.at[i],
            recv_sem=pair_recv.at[i],
            device_id={"tp": 1 - core},
            device_id_type=pl.DeviceIdType.MESH,
        )

    for j in range(PIECES):
        pieces[2 * j].wait()
        part_k[j] = dot(tok[...], key[j])
        pieces[2 * j + 1].wait()
        part_v[j] = dot(tok[...], value[j])
        if j == PIECES // 2 - 1:
            pair(0).start()
            pair(1).start()
            loads[2].wait()
            low_ref[...] = jnp.zeros_like(low_ref)

            def add_low(a, carry):
                low = dot(tok[...], down[a])
                low_ref[...] = jnp.where(idx_ref[...] == a, low, low_ref[...])
                return carry

            lax.fori_loop(0, slots, add_low, 0)
            pair(2).start()
    loads[3].wait()
    for i in range(3):
        pair(i).wait()
    low = (low_ref[...] + got_low[...]).astype(BF16)
    rank = low.shape[1] // 2
    idx = idx_ref[...]
    parts = [jnp.where(idx == s, low, jnp.zeros_like(low)) for s in range(slots)]
    for kind, (mine, got) in enumerate([(part_k, got_k), (part_v, got_vv)]):
        for j in range(PIECES // 2):
            total = mine[PIECES // 2 + j] + got[j]
            for s in range(slots):
                total += dot(
                    parts[s][:, kind * rank : (kind + 1) * rank],
                    up[s, kind, :, j * tile : (j + 1) * tile],
                )
            start = kind * width + j * tile
            fresh[:, start : start + tile] = total.astype(BF16)

    rows = QUERY_GROUP * steps_t * NB
    half = rows // 2
    old_lanes = context * NB
    new_lanes = steps_t * NB
    factor = HEAD_SIZE ** (-0.5)
    dims = (((1,), (1,)), ((), ()))
    loads[4].wait()

    def weigh(b, carry):
        here = pl.ds(pl.multiple_of(b * NB, NB), NB)
        row, lane = iota((rows, old_lanes), 0), iota((rows, old_lanes), 1)
        old_ok = (row % NB == lane % NB) & (valid_ref[b] > 0)
        row, lane = iota((rows, new_lanes), 0), iota((rows, new_lanes), 1)
        new_ok = (row % NB == lane % NB) & (lane // NB <= (row // NB) % steps_t)
        q = query[:, here, :].reshape(steps_t * NB, query.shape[2])
        k = keys[here, :]
        new_k = jnp.concatenate(
            [
                fresh[pl.ds(pl.multiple_of(t * requests + b * NB, NB), NB), :width]
                for t in range(steps_t)
            ],
            axis=0,
        )
        total = jnp.zeros((half, 128), F32)
        for g in range(heads):
            start = g * QUERY_GROUP * HEAD_SIZE
            qg = jnp.concatenate(
                [q[:, start + h * HEAD_SIZE : start + (h + 1) * HEAD_SIZE] for h in range(QUERY_GROUP)],
                axis=0,
            )
            at = g * HEAD_SIZE
            kg = jnp.concatenate(
                [k[:, p * width + at : p * width + at + HEAD_SIZE] for p in range(context)], axis=0
            )
            ng = new_k[:, at : at + HEAD_SIZE]
            old = lax.dot_general(qg, kg, dims, preferred_element_type=F32) * factor
            new = lax.dot_general(qg, ng, dims, preferred_element_type=F32) * factor
            old = jnp.where(old_ok, old, -jnp.inf)
            new = jnp.where(new_ok, new, -jnp.inf)
            top = jnp.maximum(
                jnp.max(old, axis=1, keepdims=True), jnp.max(new, axis=1, keepdims=True)
            )
            old = jnp.exp(old - top)
            new = jnp.exp(new - top)
            norm = jnp.sum(old, axis=1, keepdims=True) + jnp.sum(new, axis=1, keepdims=True)
            scale = 1.0 / norm
            old = (old * scale).astype(BF16)
            new = (new * scale).astype(BF16)
            for part in range(2):
                base = part * 64 + g * LANE
                span = slice(part * half, (part + 1) * half)
                total += dot(old[span], fold_matrix(old_lanes, NB, 0, base))
                total += dot(new[span], fold_matrix(new_lanes, NB, context, base))
        total = total.astype(BF16)
        for i in range(half // NB):
            wts[here, i * 128 : (i + 1) * 128] = total[i * NB : (i + 1) * NB]
        return carry

    lax.fori_loop(0, requests // NB, weigh, 0)

    chunk = 2 * width
    for t in range(steps_t):
        place(
            fresh[t * requests : (t + 1) * requests, :], sent_s, slice(t * chunk, (t + 1) * chunk)
        )
    place(wts[...], sent_s, slice(steps_t * chunk, steps_t * chunk + wts.shape[1]))
    for k in range(1, n):
        outgoing(1, k).start()

    rows = QUERY_GROUP * steps_t * SEG
    lanes = (context + steps_t) * SEG

    def serve(v_ref, s_ref, source):
        own = iota((rows, lanes), 0) % SEG == iota((rows, lanes), 1) % SEG
        spread_r = iota((128, lanes), 0)
        spread_c = iota((128, lanes), 1) // SEG
        v = v_ref[source].astype(F32)
        s = s_ref[source].astype(F32)
        w = [
            s[:, steps_t * chunk + i * 128 : steps_t * chunk + (i + 1) * 128]
            for i in range(QUERY_GROUP * steps_t // 2)
        ]
        w = jnp.concatenate(w, axis=0).astype(BF16)
        r2, c2 = iota((2 * SEG, 2 * SEG), 0), iota((2 * SEG, 2 * SEG), 1)
        weave = (c2 == (r2 % 2) * SEG + r2 // 2).astype(BF16)
        for t in range(steps_t):
            both = [s[:, t * chunk + i * width : t * chunk + (i + 1) * width] for i in range(2)]
            both = dot(weave, jnp.concatenate(both, axis=0).astype(BF16))
            kv_ref[t, source] = both.reshape(SEG, 2, width).astype(BF16)
        for g in range(heads):
            at = g * HEAD_SIZE
            vg = [v[:, p * width + at : p * width + at + HEAD_SIZE] for p in range(context)]
            for t in range(steps_t):
                start = t * chunk + width + at
                vg.append(s[:, start : start + HEAD_SIZE])
            vg = jnp.concatenate(vg, axis=0).astype(BF16)
            wide = []
            for part in range(2):
                spread = (spread_r == part * 64 + g * LANE + spread_c).astype(BF16)
                wide.append(dot(w, spread))
            wide = jnp.where(own, jnp.concatenate(wide, axis=0), 0.0).astype(BF16)
            res = dot(wide, vg)
            for h in range(QUERY_GROUP):
                start = (g * QUERY_GROUP + h) * HEAD_SIZE
                for t in range(steps_t):
                    at_row = (h * steps_t + t) * SEG
                    out_ref[t, source, :, start : start + HEAD_SIZE] = res[
                        at_row : at_row + SEG
                    ].astype(BF16)

    serve(sent_v, sent_s, me)

    def arrive(k):
        incoming(0, k).wait_recv()
        incoming(1, k).wait_recv()
        serve(got_v, got_s, lax.rem(me - k + n, n))

    def step(k, carry):
        arrive(k)
        return carry

    lax.fori_loop(1, n, step, 0)
    for i in range(2):
        for k in range(1, n):
            outgoing(i, k).wait_send()


def on_device(
    tokens,
    queries,
    key_value_cache,
    key_value_length,
    request_adapter_index,
    adapter_destination,
    key_matrix,
    value_matrix,
    adapter_down_maps,
    adapter_up_maps,
):
    slots, depth, rank = adapter_down_maps.shape
    requests = request_adapter_index.shape[0]
    steps_t = tokens.shape[0]
    rows = steps_t * requests
    _, context, _, width = key_value_cache.shape
    query_width = queries.shape[2]
    n = lax.axis_size("inst")
    own_index = lax.axis_index("inst")
    chosen = request_adapter_index[:, 0]
    leaving = lax.dynamic_slice_in_dim(adapter_destination, own_index * slots, slots)
    valid = jnp.arange(context)[None, :, None] < key_value_length.reshape(-1, 1, NB)
    valid = valid.astype(jnp.int32).reshape(-1, 1, context * NB)
    idx = jnp.tile(chosen, steps_t)[:, None]
    packed = QUERY_GROUP * steps_t // 2 * 128
    second = steps_t * 2 * width + packed
    tile = key_matrix.shape[1] // PIECES
    vmem = pl.BlockSpec(memory_space=pltpu.VMEM)
    hbm = pl.BlockSpec(memory_space=pl.ANY)
    dma = pltpu.SemaphoreType.DMA
    attended, new_kv = pl.pallas_call(
        functools.partial(kernel, n, steps_t),
        in_specs=[pl.BlockSpec(memory_space=pltpu.SMEM)] + [vmem] * 4 + [hbm] * 7,
        out_specs=[vmem, vmem],
        out_shape=[
            jax.ShapeDtypeStruct((steps_t, n, SEG, query_width), BF16),
            jax.ShapeDtypeStruct((steps_t, n, SEG, 2, width), BF16),
        ],
        scratch_shapes=[
            pltpu.VMEM((requests * context * 2, width), BF16),
            pltpu.VMEM((rows, depth), BF16),
            pltpu.VMEM((PIECES, depth, tile), BF16),
            pltpu.VMEM((PIECES, depth, tile), BF16),
            pltpu.VMEM(adapter_down_maps.shape, BF16),
            pltpu.VMEM(adapter_up_maps.shape, BF16),
            pltpu.VMEM(queries.shape, BF16),
            pltpu.VMEM((n * SEG, requests), BF16),
            pltpu.VMEM((requests, context * width), BF16),
            pltpu.VMEM((requests, context * width), BF16),
            pltpu.VMEM((n, SEG, context * width), BF16),
            pltpu.VMEM((n, SEG, context * width), BF16),
            pltpu.VMEM((n, SEG, second), BF16),
            pltpu.VMEM((n, SEG, second), BF16),
            pltpu.VMEM((PIECES, rows, tile), F32),
            pltpu.VMEM((PIECES, rows, tile), F32),
            pltpu.VMEM((PIECES // 2, rows, tile), F32),
            pltpu.VMEM((PIECES // 2, rows, tile), F32),
            pltpu.VMEM((rows, rank), F32),
            pltpu.VMEM((rows, rank), F32),
            pltpu.VMEM((rows, 2 * width), BF16),
            pltpu.VMEM((requests, packed), BF16),
            dma((5,)),
            dma((2, PIECES)),
            dma((3,)),
            dma((3,)),
            dma((2, n)),
            dma((2, n)),
        ],
        compiler_params=pltpu.CompilerParams(
            collective_id=0, has_side_effects=True, vmem_limit_bytes=VMEM_LIMIT
        ),
        name="migrate",
    )(
        leaving, chosen[None, :], chosen[:, None], idx, valid,
        key_value_cache.reshape(-1, width), tokens.reshape(rows, depth), key_matrix, value_matrix,
        adapter_down_maps, adapter_up_maps, queries,
    )
    if n != slots:
        coming = adapter_destination.reshape(n, slots) == own_index
        coming = jnp.sum(coming.astype(jnp.int32), axis=1)
        hit = coming[None, :] * (jnp.cumsum(coming)[None, :] - 1 == jnp.arange(slots)[:, None])
        anchor = jnp.sum(hit * jnp.arange(n)[None, :], axis=1)
        attended = jnp.take(attended, anchor, axis=1)
        new_kv = jnp.take(new_kv, anchor, axis=1)
    return (
        attended.reshape(steps_t, slots * SEG, query_width),
        new_kv.reshape(steps_t, slots * SEG, 2, width),
    )


def solution(mesh):
    return jax.shard_map(
        on_device,
        mesh=mesh,
        in_specs=(
            P(None, ("grp", "inst"), "tp"),
            P(None, ("grp", "inst"), "tp"),
            P(("grp", "inst"), None, None, "tp"),
            P(("grp", "inst")),
            P(("grp", "inst"), None),
            P("grp"),
            P("tp", None),
            P("tp", None),
            P(("grp", "inst"), "tp", None),
            P(("grp", "inst"), None, None, "tp"),
        ),
        out_specs=(P(None, ("grp", "inst"), "tp"), P(None, ("grp", "inst"), None, "tp")),
        check_vma=False,
    )
```

time: 420 us -> 88.3 us (0.21)
  the two profiles are of different devices: /device:TPU:0 before, /device:TPU:28 now
where the time goes in v3:
time: 88.3 us; the launch traced here: 88 us
  Pallas kernels  71.6 us (81%)
  local copies, waits for them, and re-layouts  15.2 us (17%)
    pallas_call x1, Pallas kernels, on_device(): pl.pallas_call(functools.partial(kernel, n, steps_t), in_specs=[pl.BlockS...  71.6 us
    unnamed x5, local copies, waits for them, and re-layouts  6.28 us
    reshape x1, local copies, waits for them, and re-layouts, on_device(): key_value_cache.reshape(-1, width)  5.1 us

profile of v3, /device:TPU:28, one launch (start us, length us, event | category | flops | bytes accessed | tf_op | source)
XLA Modules:
  0.0 88.0 jit_solution(11854707517155646853)
XLA Ops:
  0.6 1.3 %dynamic_slice.3.leaving_ref = s32[8]{0:T(128)} dynamic-slice(s32[64]{0:T(128)} %param.15, s32[]{:T(128)S(6)} %select_n.3), dynamic_slice_sizes={8} | dynamic-slice | bytes 68 | tf_op jit(solution)/shard_map/dynamic_slice | solution.py:349
  1.9 0.7 tile.8
  2.6 0.1 lt.33
  2.7 0.8 lt.35
  3.5 0.1 lt.37
  3.6 0.6 compare_convert_fusion.valid_ref
  4.2 1.4 %copy.13.col_ref = s32[160,1]{1,0:T(8,128)} copy(s32[160,1]{0,1:T(1,128)} %param.14) | data formatting | bytes 1280 | tf_op args[4]
  5.6 0.9 broadcast_in_dim_tile.4.idx_ref
  6.5 5.1 %reshape.57.cache_hbm = bf16[2560,512]{1,0:T(8,128)(2,1)} reshape(bf16[160,8,2,512]{3,2,1,0:T(2,128)(2,1)} %param.12) | data formatting | bytes 5242880 | tf_op jit(solution)/shard_map/reshape | solution.py:403
  11.6 71.6 %migrate.1 = (bf16[2,8,24,4096]{3,2,1,0:T(8,128)(2,1)}, bf16[2,8,24,2,512]{4,3,2,1,0:T(2,128)(2,1)}) custom-call(s32[8]{0:T(128)} %dynamic_slice.3.leaving_ref, s32[1,160]{1,0:T(1,128)} %bitcast.9, s32[160,1]{1,0:T(8,128)} %copy.13.col_ref, s32[320,1]{1,0:T(8,128)} %broadcast_in_dim_tile.4.idx_ref, s32[10,1,128]{2,1,0:T(1,128)} %compare_convert_fusion.valid_ref, ...), custom_call_target="tpu_custom_call" | custom-call | tf_op jit(solution)/shard_map/migrate/pallas_call | solution.py:359
  83.2 0.0 copy-start
  83.2 4.0 %copy.17 = bf16[2,192,4096]{2,1,0:T(8,128)(2,1)} copy(bf16[2,192,4096]{2,1,0:T(8,128)(2,1)} %bitcast.5) | data formatting | bytes 6291456
  87.1 0.0 copy-done
  87.2 0.9 copy.18
  (2 shorter events, 0.0 us)
Async XLA Ops:
  83.2 4.0 %copy-start = (bf16[2,8,24,2,512]{4,3,2,1,0:T(2,128)(2,1)S(1)}, bf16[2,8,24,2,512]{4,3,2,1,0:T(2,128)(2,1)}, u32[]{:S(2)}) copy-start(bf16[2,8,24,2,512]{4,3,2,1,0:T(2,128)(2,1)} %get-tuple-element.5) | copy-start | bytes 2359300

commit v4 on v3

--- a/solution.py
+++ b/solution.py
@@ -13,7 +13,7 @@
 NB = 16
 LANE = 16
 PIECES = 4
-VMEM_LIMIT = 56 * 1024 * 1024
+MIB = 1024 * 1024
 F32 = jnp.float32
 BF16 = jnp.bfloat16
 
@@ -32,18 +32,17 @@
 
 def kernel(
     n, steps_t,
-    leaving_ref, row_ref, col_ref, idx_ref, valid_ref,
+    leaving_ref, row_ref, length_ref,
     cache_hbm, tok_hbm, key_hbm, value_hbm, down_hbm, up_hbm, query_hbm,
     out_ref, kv_ref,
     cache, tok, key, value, down, up, query,
     pick_ref, vals, keys, sent_v, got_v, sent_s, got_s,
     part_k, part_v, got_k, got_vv, low_ref, got_low, fresh, wts,
-    load_sem, piece_sem, pair_send, pair_recv, send_sem, recv_sem,
+    idx_ref, len_ref, load_sem, piece_sem, pair_send, pair_recv, send_sem, recv_sem,
 ):
     me = lax.axis_index("inst")
     core = lax.axis_index("tp")
-    requests = col_ref.shape[0]
-    width = cache.shape[1]
+    requests, _, _, width = cache.shape
     context = vals.shape[1] // width
     heads = width // HEAD_SIZE
     slots = down.shape[0]
@@ -70,10 +69,17 @@
     for load in loads[2:]:
         load.start()
 
+    def partner(k):
+        total, bit = 0, 1
+        while bit < n:
+            total += lax.rem(me // bit + k // bit, 2) * bit
+            bit *= 2
+        return total
+
     barrier = pltpu.get_barrier_semaphore()
     for k in range(1, n):
         pl.semaphore_signal(
-            barrier, inc=1, device_id={"inst": lax.rem(me + k, n)},
+            barrier, inc=1, device_id={"inst": partner(k)},
             device_id_type=pl.DeviceIdType.MESH,
         )
     pl.semaphore_signal(
@@ -83,10 +89,14 @@
     chosen = row_ref[...]
     r = iota((requests, requests), 0)
     c = iota((requests, requests), 1)
-    same = jnp.where((col_ref[...] == chosen) & (r < c), 1, 0)
+    column = jnp.sum(jnp.where(r == c, chosen, 0), axis=1, keepdims=True)
+    for t in range(steps_t):
+        idx_ref[t * requests : (t + 1) * requests] = column
+    len_ref[...] = jnp.sum(jnp.where(r == c, length_ref[...], 0), axis=1, keepdims=True)
+    same = jnp.where((column == chosen) & (r < c), 1, 0)
     seat = jnp.sum(same, axis=0, keepdims=True)
     for a in range(slots):
-        seat += jnp.where(chosen == a, leaving_ref[a] * SEG, 0)
+        seat += jnp.where(chosen == a, leaving_ref[me * slots + a] * SEG, 0)
     pick_ref[...] = (iota((n * SEG, requests), 0) == seat).astype(BF16)
 
     block = 2 * context * NB
@@ -99,7 +109,7 @@
 
     def split(take, into):
         def body(b, carry):
-            x = cache[pl.ds(pl.multiple_of(b * block, block), block)]
+            x = cache[pl.ds(b * NB, NB)].reshape(block, width)
             v = dot(take, x).astype(BF16)
             here = pl.ds(pl.multiple_of(b * NB, NB), NB)
             for p in range(context):
@@ -123,7 +133,7 @@
 
     def outgoing(i, k):
         src, dst = [(sent_v, got_v), (sent_s, got_s)][i]
-        to = lax.rem(me + k, n)
+        to = partner(k)
         return pltpu.make_async_remote_copy(
             src_ref=src.at[to],
             dst_ref=dst.at[me],
@@ -135,7 +145,7 @@
 
     def incoming(i, k):
         src, dst = [(sent_v, got_v), (sent_s, got_s)][i]
-        source = lax.rem(me - k + n, n)
+        source = partner(k)
         return pltpu.make_async_remote_copy(
             src_ref=src.at[source],
             dst_ref=dst.at[source],
@@ -145,8 +155,17 @@
             device_id_type=pl.DeviceIdType.MESH,
         )
 
-    for k in range(1, n):
-        outgoing(0, k).start()
+    turn = n // 2 - lax.rem(me // 2, 2) * 2 - core
+
+    def send(i):
+        def one(j, carry):
+            m = lax.rem(j + turn, n - 1)
+            outgoing(i, lax.rem(n // 2 + m + m // (n // 2), n)).start()
+            return carry
+
+        lax.fori_loop(0, n - 1, one, 0)
+
+    send(0)
     split(take_key, keys)
 
     loads[1].wait()
@@ -209,7 +228,8 @@
     def weigh(b, carry):
         here = pl.ds(pl.multiple_of(b * NB, NB), NB)
         row, lane = iota((rows, old_lanes), 0), iota((rows, old_lanes), 1)
-        old_ok = (row % NB == lane % NB) & (valid_ref[b] > 0)
+        live = jnp.concatenate([len_ref[here, :]] * (QUERY_GROUP * steps_t), axis=0)
+        old_ok = (row % NB == lane % NB) & (lane // NB < live)
         row, lane = iota((rows, new_lanes), 0), iota((rows, new_lanes), 1)
         new_ok = (row % NB == lane % NB) & (lane // NB <= (row // NB) % steps_t)
         q = query[:, here, :].reshape(steps_t * NB, query.shape[2])
@@ -264,8 +284,7 @@
             fresh[t * requests : (t + 1) * requests, :], sent_s, slice(t * chunk, (t + 1) * chunk)
         )
     place(wts[...], sent_s, slice(steps_t * chunk, steps_t * chunk + wts.shape[1]))
-    for k in range(1, n):
-        outgoing(1, k).start()
+    send(1)
 
     rows = QUERY_GROUP * steps_t * SEG
     lanes = (context + steps_t) * SEG
@@ -313,7 +332,7 @@
     def arrive(k):
         incoming(0, k).wait_recv()
         incoming(1, k).wait_recv()
-        serve(got_v, got_s, lax.rem(me - k + n, n))
+        serve(got_v, got_s, partner(k))
 
     def step(k, carry):
         arrive(k)
@@ -344,28 +363,22 @@
     _, context, _, width = key_value_cache.shape
     query_width = queries.shape[2]
     n = lax.axis_size("inst")
-    own_index = lax.axis_index("inst")
-    chosen = request_adapter_index[:, 0]
-    leaving = lax.dynamic_slice_in_dim(adapter_destination, own_index * slots, slots)
-    valid = jnp.arange(context)[None, :, None] < key_value_length.reshape(-1, 1, NB)
-    valid = valid.astype(jnp.int32).reshape(-1, 1, context * NB)
-    idx = jnp.tile(chosen, steps_t)[:, None]
     packed = QUERY_GROUP * steps_t // 2 * 128
     second = steps_t * 2 * width + packed
     tile = key_matrix.shape[1] // PIECES
     vmem = pl.BlockSpec(memory_space=pltpu.VMEM)
-    hbm = pl.BlockSpec(memory_space=pl.ANY)
+    hbm = pl.BlockSpec(memory_space=pltpu.MemorySpace.HBM)
     dma = pltpu.SemaphoreType.DMA
     attended, new_kv = pl.pallas_call(
         functools.partial(kernel, n, steps_t),
-        in_specs=[pl.BlockSpec(memory_space=pltpu.SMEM)] + [vmem] * 4 + [hbm] * 7,
+        in_specs=[pl.BlockSpec(memory_space=pltpu.SMEM)] + [vmem] * 2 + [hbm] * 7,
         out_specs=[vmem, vmem],
         out_shape=[
             jax.ShapeDtypeStruct((steps_t, n, SEG, query_width), BF16),
             jax.ShapeDtypeStruct((steps_t, n, SEG, 2, width), BF16),
         ],
         scratch_shapes=[
-            pltpu.VMEM((requests * context * 2, width), BF16),
+            pltpu.VMEM(key_value_cache.shape, BF16),
             pltpu.VMEM((rows, depth), BF16),
             pltpu.VMEM((PIECES, depth, tile), BF16),
             pltpu.VMEM((PIECES, depth, tile), BF16),
@@ -387,6 +400,8 @@
             pltpu.VMEM((rows, rank), F32),
             pltpu.VMEM((rows, 2 * width), BF16),
             pltpu.VMEM((requests, packed), BF16),
+            pltpu.VMEM((rows, 1), jnp.int32),
+            pltpu.VMEM((requests, 1), jnp.int32),
             dma((5,)),
             dma((2, PIECES)),
             dma((3,)),
@@ -395,16 +410,16 @@
             dma((2, n)),
         ],
         compiler_params=pltpu.CompilerParams(
-            collective_id=0, has_side_effects=True, vmem_limit_bytes=VMEM_LIMIT
+            collective_id=0, has_side_effects=True, vmem_limit_bytes=(32 + n) * MIB
         ),
         name="migrate",
     )(
-        leaving, chosen[None, :], chosen[:, None], idx, valid,
-        key_value_cache.reshape(-1, width), tokens.reshape(rows, depth), key_matrix, value_matrix,
+        adapter_destination, request_adapter_index.reshape(1, requests),
+        key_value_length.reshape(1, requests), key_value_cache, tokens.reshape(rows, depth), key_matrix, value_matrix,
         adapter_down_maps, adapter_up_maps, queries,
     )
     if n != slots:
-        coming = adapter_destination.reshape(n, slots) == own_index
+        coming = adapter_destination.reshape(n, slots) == lax.axis_index("inst")
         coming = jnp.sum(coming.astype(jnp.int32), axis=1)
         hit = coming[None, :] * (jnp.cumsum(coming)[None, :] - 1 == jnp.arange(slots)[:, None])
         anchor = jnp.sum(hit * jnp.arange(n)[None, :], axis=1)

time: 88.3 us -> 80.3 us (0.909)
  the two profiles are of different devices: /device:TPU:28 before, /device:TPU:24 now
where the time goes in v4:
time: 80.3 us; the launch traced here: 80 us
  Pallas kernels  68.8 us (86%)
  local copies, waits for them, and re-layouts  10.6 us (13%)
    pallas_call x1, Pallas kernels, on_device(): pl.pallas_call(functools.partial(kernel, n, steps_t), in_specs=[pl.BlockS...  68.8 us
    unnamed x16, local copies, waits for them, and re-layouts  10.6 us

profile of v4, /device:TPU:24, one launch (start us, length us, event | category | flops | bytes accessed | tf_op | source)
XLA Modules:
  0.0 80.0 jit_solution(16482780101635737986)
XLA Ops:
  0.6 0.0 copy-start
  0.6 1.7 %copy-done = bf16[160,8,2,512]{3,2,1,0:T(2,128)(2,1)S(1)} copy-done((bf16[160,8,2,512]{3,2,1,0:T(2,128)(2,1)S(1)}, bf16[160,8,2,512]{3,2,1,0:T(2,128)(2,1)}, u32[]{:S(2)}) %copy-start) | copy-done | bytes 2621464
  2.4 0.0 copy-start.1
  2.4 1.7 %copy-done.1 = bf16[2,160,4096]{2,1,0:T(8,128)(2,1)S(1)} copy-done((bf16[2,160,4096]{2,1,0:T(8,128)(2,1)S(1)}, bf16[2,160,4096]{2,1,0:T(8,128)(2,1)}, u32[]{:S(2)}) %copy-start.1) | copy-done | bytes 2621464
  4.1 0.0 copy-start.2
  4.1 1.3 %copy-done.2 = bf16[2,160,2048]{2,1,0:T(8,128)(2,1)S(1)} copy-done((bf16[2,160,2048]{2,1,0:T(8,128)(2,1)S(1)}, bf16[2,160,2048]{2,1,0:T(8,128)(2,1)}, u32[]{:S(2)}) %copy-start.2) | copy-done | bytes 1310744
  5.4 0.0 copy-start.3
  5.4 1.2 %copy-done.3 = bf16[8,2,64,512]{3,2,1,0:T(8,128)(2,1)S(1)} copy-done((bf16[8,2,64,512]{3,2,1,0:T(8,128)(2,1)S(1)}, bf16[8,2,64,512]{3,2,1,0:T(8,128)(2,1)}, u32[]{:S(2)}) %copy-start.3) | copy-done | bytes 1048600
  6.7 0.0 copy-start.4
  6.7 0.7 copy-done.4
  7.3 0.0 copy-start.5
  7.3 0.7 copy-done.5
  8.0 0.0 copy-start.6
  8.0 0.7 copy-done.6
  8.7 68.8 %migrate.1 = (bf16[2,8,24,4096]{3,2,1,0:T(8,128)(2,1)S(1)}, bf16[2,8,24,2,512]{4,3,2,1,0:T(2,128)(2,1)S(1)}) custom-call(s32[64]{0:T(128)S(1)} %copy-done.6, s32[1,160]{1,0:T(1,128)S(1)} %bitcast.8, s32[1,160]{1,0:T(1,128)S(1)} %bitcast.9, bf16[160,8,2,512]{3,2,1,0:T(2,128)(2,1)S(1)} %copy-done, bf16[320,2048]{1,0:T(8,128)(2,1)S(1)} %bitcast.6, ...), custom_call_target="tpu_custom_call" | custom-call | tf_op jit(solution)/shard_map/migrate/pallas_call | solution.py:372
  77.5 1.7 %copy.14 = bf16[2,192,4096]{2,1,0:T(8,128)(2,1)} copy(bf16[2,192,4096]{2,1,0:T(8,128)(2,1)S(1)} %bitcast.5) | data formatting | bytes 6291456
  79.2 0.9 %copy.15 = bf16[2,192,2,512]{3,2,1,0:T(2,128)(2,1)} copy(bf16[2,192,2,512]{3,2,1,0:T(2,128)(2,1)S(1)} %bitcast.7) | data formatting | bytes 1572864
Async XLA Ops:
  0.6 1.7 %copy-start = (bf16[160,8,2,512]{3,2,1,0:T(2,128)(2,1)S(1)}, bf16[160,8,2,512]{3,2,1,0:T(2,128)(2,1)}, u32[]{:S(2)}) copy-start(bf16[160,8,2,512]{3,2,1,0:T(2,128)(2,1)} %cache_hbm.1) | copy-start | bytes 7864324
  2.4 1.7 %copy-start.1 = (bf16[2,160,4096]{2,1,0:T(8,128)(2,1)S(1)}, bf16[2,160,4096]{2,1,0:T(8,128)(2,1)}, u32[]{:S(2)}) copy-start(bf16[2,160,4096]{2,1,0:T(8,128)(2,1)} %query_hbm.1) | copy-start | bytes 7864324
  4.1 1.3 %copy-start.2 = (bf16[2,160,2048]{2,1,0:T(8,128)(2,1)S(1)}, bf16[2,160,2048]{2,1,0:T(8,128)(2,1)}, u32[]{:S(2)}) copy-start(bf16[2,160,2048]{2,1,0:T(8,128)(2,1)} %param.10) | copy-start | bytes 3932164
  5.4 1.2 %copy-start.3 = (bf16[8,2,64,512]{3,2,1,0:T(8,128)(2,1)S(1)}, bf16[8,2,64,512]{3,2,1,0:T(8,128)(2,1)}, u32[]{:S(2)}) copy-start(bf16[8,2,64,512]{3,2,1,0:T(8,128)(2,1)} %up_hbm.1) | copy-start | bytes 3145732
  6.7 0.7 copy-start.4
  7.3 0.7 copy-start.5
  8.0 0.7 copy-start.6

commit v5 on v4

--- a/solution.py
+++ b/solution.py
@@ -11,7 +11,6 @@
 HEAD_SIZE = 128
 SEG = 24
 NB = 16
-LANE = 16
 PIECES = 4
 MIB = 1024 * 1024
 F32 = jnp.float32
@@ -24,10 +23,6 @@
 
 def iota(shape, axis):
     return lax.broadcasted_iota(jnp.int32, shape, axis)
-
-
-def fold_matrix(rows, n_of, p_base, lane_base):
-    return (iota((rows, 128), 1) == lane_base + p_base + iota((rows, 128), 0) // n_of).astype(BF16)
 
 
 def kernel(
@@ -218,7 +213,7 @@
             fresh[:, start : start + tile] = total.astype(BF16)
 
     rows = QUERY_GROUP * steps_t * NB
-    half = rows // 2
+    near = 128 // (heads * context)
     old_lanes = context * NB
     new_lanes = steps_t * NB
     factor = HEAD_SIZE ** (-0.5)
@@ -241,7 +236,13 @@
             ],
             axis=0,
         )
-        total = jnp.zeros((half, 128), F32)
+        total = jnp.zeros((rows, 128), F32)
+        total_new = jnp.zeros((rows, 128), F32)
+        row, lane = iota((rows, 128), 0) // NB, iota((rows, 128), 1)
+        fold_old = iota((old_lanes, 128), 1) % context == iota((old_lanes, 128), 0) // NB
+        fold_old = fold_old.astype(BF16)
+        fold_new = iota((new_lanes, 128), 1) % steps_t == iota((new_lanes, 128), 0) // NB
+        fold_new = fold_new.astype(BF16)
         for g in range(heads):
             start = g * QUERY_GROUP * HEAD_SIZE
             qg = jnp.concatenate(
@@ -266,14 +267,16 @@
             scale = 1.0 / norm
             old = (old * scale).astype(BF16)
             new = (new * scale).astype(BF16)
-            for part in range(2):
-                base = part * 64 + g * LANE
-                span = slice(part * half, (part + 1) * half)
-                total += dot(old[span], fold_matrix(old_lanes, NB, 0, base))
-                total += dot(new[span], fold_matrix(new_lanes, NB, context, base))
-        total = total.astype(BF16)
-        for i in range(half // NB):
-            wts[here, i * 128 : (i + 1) * 128] = total[i * NB : (i + 1) * NB]
+            here_old = lane // context == (row // steps_t) % near * heads + g
+            total = jnp.where(here_old, dot(old, fold_old), total)
+            total_new = jnp.where(lane // steps_t == row * heads + g, dot(new, fold_new), total_new)
+        tiles = QUERY_GROUP // near * steps_t
+        for i in range(tiles):
+            first = i // steps_t * near * steps_t + i % steps_t
+            piece = [total[j * NB : (j + 1) * NB] for j in range(first, first + near * steps_t, steps_t)]
+            wts[here, i * 128 : (i + 1) * 128] = sum(piece[1:], piece[0]).astype(BF16)
+        piece = [total_new[j * NB : (j + 1) * NB] for j in range(QUERY_GROUP * steps_t)]
+        wts[here, tiles * 128 : (tiles + 1) * 128] = sum(piece[1:], piece[0]).astype(BF16)
         return carry
 
     lax.fori_loop(0, requests // NB, weigh, 0)
@@ -291,15 +294,23 @@
 
     def serve(v_ref, s_ref, source):
         own = iota((rows, lanes), 0) % SEG == iota((rows, lanes), 1) % SEG
-        spread_r = iota((128, lanes), 0)
-        spread_c = iota((128, lanes), 1) // SEG
+        r, c = iota((256, lanes), 0), iota((256, lanes), 1) // SEG
+        spread = ((r < 128) & (r % context == c)) | ((r >= 128) & (context + r % steps_t == c))
+        spread = spread.astype(BF16)
+        row, lane = iota((rows, 128), 0) // SEG, iota((rows, 128), 1)
+        old_at = lane // context - (row // steps_t) % near * heads
+        new_at = lane // steps_t - row * heads
         v = v_ref[source].astype(F32)
         s = s_ref[source].astype(F32)
         w = [
             s[:, steps_t * chunk + i * 128 : steps_t * chunk + (i + 1) * 128]
-            for i in range(QUERY_GROUP * steps_t // 2)
+            for i in range(QUERY_GROUP // near * steps_t + 1)
         ]
-        w = jnp.concatenate(w, axis=0).astype(BF16)
+        w_old = [
+            w[h // near * steps_t + t] for h in range(QUERY_GROUP) for t in range(steps_t)
+        ]
+        w_old = jnp.concatenate(w_old, axis=0)
+        w_new = jnp.concatenate([w[-1]] * (QUERY_GROUP * steps_t), axis=0)
         r2, c2 = iota((2 * SEG, 2 * SEG), 0), iota((2 * SEG, 2 * SEG), 1)
         weave = (c2 == (r2 % 2) * SEG + r2 // 2).astype(BF16)
         for t in range(steps_t):
@@ -313,11 +324,9 @@
                 start = t * chunk + width + at
                 vg.append(s[:, start : start + HEAD_SIZE])
             vg = jnp.concatenate(vg, axis=0).astype(BF16)
-            wide = []
-            for part in range(2):
-                spread = (spread_r == part * 64 + g * LANE + spread_c).astype(BF16)
-                wide.append(dot(w, spread))
-            wide = jnp.where(own, jnp.concatenate(wide, axis=0), 0.0).astype(BF16)
+            mine = [jnp.where(old_at == g, w_old, 0.0), jnp.where(new_at == g, w_new, 0.0)]
+            wide = dot(jnp.concatenate(mine, axis=1).astype(BF16), spread)
+            wide = jnp.where(own, wide, 0.0).astype(BF16)
             res = dot(wide, vg)
             for h in range(QUERY_GROUP):
                 start = (g * QUERY_GROUP + h) * HEAD_SIZE
@@ -363,7 +372,7 @@
     _, context, _, width = key_value_cache.shape
     query_width = queries.shape[2]
     n = lax.axis_size("inst")
-    packed = QUERY_GROUP * steps_t // 2 * 128
+    packed = QUERY_GROUP * steps_t * (width // HEAD_SIZE) * (context + steps_t)
     second = steps_t * 2 * width + packed
     tile = key_matrix.shape[1] // PIECES
     vmem = pl.BlockSpec(memory_space=pltpu.VMEM)

time: 80.3 us -> 77.6 us (0.966)
  Pallas kernels: 68.8 us -> 66.1 us
    pallas_call x1, Pallas kernels: 68.8 us -> 66.1 us  [on_device(): pl.pallas_call(functools.partial(kernel, n, steps_t), in_specs=[pl.BlockS...]
where the time goes in v5:
time: 77.6 us; the launch traced here: 77.3 us
  Pallas kernels  66.1 us (85%)
  local copies, waits for them, and re-layouts  10.6 us (14%)
    pallas_call x1, Pallas kernels, on_device(): pl.pallas_call(functools.partial(kernel, n, steps_t), in_specs=[pl.BlockS...  66.1 us
    unnamed x16, local copies, waits for them, and re-layouts  10.6 us

profile of v5, /device:TPU:24, one launch (start us, length us, event | category | flops | bytes accessed | tf_op | source)
XLA Modules:
  0.0 77.3 jit_solution(7712228451918608794)
XLA Ops:
  0.6 0.0 copy-start
  0.6 1.7 %copy-done = bf16[160,8,2,512]{3,2,1,0:T(2,128)(2,1)S(1)} copy-done((bf16[160,8,2,512]{3,2,1,0:T(2,128)(2,1)S(1)}, bf16[160,8,2,512]{3,2,1,0:T(2,128)(2,1)}, u32[]{:S(2)}) %copy-start) | copy-done | bytes 2621464
  2.4 0.0 copy-start.1
  2.4 1.7 %copy-done.1 = bf16[2,160,4096]{2,1,0:T(8,128)(2,1)S(1)} copy-done((bf16[2,160,4096]{2,1,0:T(8,128)(2,1)S(1)}, bf16[2,160,4096]{2,1,0:T(8,128)(2,1)}, u32[]{:S(2)}) %copy-start.1) | copy-done | bytes 2621464
  4.1 0.0 copy-start.2
  4.1 1.3 %copy-done.2 = bf16[2,160,2048]{2,1,0:T(8,128)(2,1)S(1)} copy-done((bf16[2,160,2048]{2,1,0:T(8,128)(2,1)S(1)}, bf16[2,160,2048]{2,1,0:T(8,128)(2,1)}, u32[]{:S(2)}) %copy-start.2) | copy-done | bytes 1310744
  5.4 0.0 copy-start.3
  5.4 1.2 %copy-done.3 = bf16[8,2,64,512]{3,2,1,0:T(8,128)(2,1)S(1)} copy-done((bf16[8,2,64,512]{3,2,1,0:T(8,128)(2,1)S(1)}, bf16[8,2,64,512]{3,2,1,0:T(8,128)(2,1)}, u32[]{:S(2)}) %copy-start.3) | copy-done | bytes 1048600
  6.7 0.0 copy-start.4
  6.7 0.7 copy-done.4
  7.3 0.0 copy-start.5
  7.3 0.7 copy-done.5
  8.0 0.0 copy-start.6
  8.0 0.7 copy-done.6
  8.7 66.1 %migrate.1 = (bf16[2,8,24,4096]{3,2,1,0:T(8,128)(2,1)S(1)}, bf16[2,8,24,2,512]{4,3,2,1,0:T(2,128)(2,1)S(1)}) custom-call(s32[64]{0:T(128)S(1)} %copy-done.6, s32[1,160]{1,0:T(1,128)S(1)} %bitcast.8, s32[1,160]{1,0:T(1,128)S(1)} %bitcast.9, bf16[160,8,2,512]{3,2,1,0:T(2,128)(2,1)S(1)} %copy-done, bf16[320,2048]{1,0:T(8,128)(2,1)S(1)} %bitcast.6, ...), custom_call_target="tpu_custom_call" | custom-call | tf_op jit(solution)/shard_map/migrate/pallas_call | solution.py:381
  74.8 1.7 %copy.14 = bf16[2,192,4096]{2,1,0:T(8,128)(2,1)} copy(bf16[2,192,4096]{2,1,0:T(8,128)(2,1)S(1)} %bitcast.5) | data formatting | bytes 6291456
  76.4 0.9 %copy.15 = bf16[2,192,2,512]{3,2,1,0:T(2,128)(2,1)} copy(bf16[2,192,2,512]{3,2,1,0:T(2,128)(2,1)S(1)} %bitcast.7) | data formatting | bytes 1572864
Async XLA Ops:
  0.6 1.7 %copy-start = (bf16[160,8,2,512]{3,2,1,0:T(2,128)(2,1)S(1)}, bf16[160,8,2,512]{3,2,1,0:T(2,128)(2,1)}, u32[]{:S(2)}) copy-start(bf16[160,8,2,512]{3,2,1,0:T(2,128)(2,1)} %cache_hbm.1) | copy-start | bytes 7864324
  2.4 1.7 %copy-start.1 = (bf16[2,160,4096]{2,1,0:T(8,128)(2,1)S(1)}, bf16[2,160,4096]{2,1,0:T(8,128)(2,1)}, u32[]{:S(2)}) copy-start(bf16[2,160,4096]{2,1,0:T(8,128)(2,1)} %query_hbm.1) | copy-start | bytes 7864324
  4.1 1.3 %copy-start.2 = (bf16[2,160,2048]{2,1,0:T(8,128)(2,1)S(1)}, bf16[2,160,2048]{2,1,0:T(8,128)(2,1)}, u32[]{:S(2)}) copy-start(bf16[2,160,2048]{2,1,0:T(8,128)(2,1)} %param.10) | copy-start | bytes 3932164
  5.4 1.2 %copy-start.3 = (bf16[8,2,64,512]{3,2,1,0:T(8,128)(2,1)S(1)}, bf16[8,2,64,512]{3,2,1,0:T(8,128)(2,1)}, u32[]{:S(2)}) copy-start(bf16[8,2,64,512]{3,2,1,0:T(8,128)(2,1)} %up_hbm.1) | copy-start | bytes 3145732
  6.7 0.7 copy-start.4
  7.3 0.7 copy-start.5
  8.0 0.7 copy-start.6
